TPU v7x, 512 devices: a whole 4x4x16 slice. The times are simulated.
512 devices in a mesh: tp: 8 (over z_hi, x), dp: 64 (over y, z_lo, core).
Axes of the slice: x: 4, y: 4, z: 16 (z_hi: 2, z_lo: 8; z = z_hi * 8 + z_lo), core: 2. Of those that a mesh axis runs over, the one named last changes fastest.
Arguments:
- features: bfloat16 [8192, 1536], P('dp', 'tp'), may hold values from -2 to 2
- proj_weight: bfloat16 [1536, 1024], P('tp'), may hold values from -0.15625 to 0.15625
- text_embed: bfloat16 [8192, 1024], P(('tp', 'dp')), may hold values from -2 to 2
- log_scale: float32 [1], replicated, may hold values from 2 to 2.6
- logit_bias: float32 [1], replicated, may hold values from -7 to -5
Outputs:
- image_grad: bfloat16 [8192, 1536], P('dp', 'tp')
- weight_grad: bfloat16 [1536, 1024], P('tp')
- text_grad: bfloat16 [8192, 1024], P(('tp', 'dp'))
All inputs are finite; a program needn't handle non-finite values.
Results may differ from a plain program's by a relative error of at most 0.0063.
Values may be sent and summed in bfloat16 or wider, within the bound.
No kernel may reach another device: no remote copies, remote signals or barrier semaphores. Data moves between devices by JAX's collectives and lax.ppermute only.
A program may use at most 64 MiB of HBM per device.

v0:
```python
import jax
import jax.numpy as jnp
from jax import lax
from jax.sharding import PartitionSpec as P


def unit_backward(grad_unit, unit_value, inverse):
    along = jnp.sum(unit_value * grad_unit, axis=1, keepdims=True)
    return inverse * (grad_unit - along * unit_value)


def shards(features, proj_weight, text_embed, log_scale, logit_bias):
    image_rows = features.shape[0]
    text_rows = text_embed.shape[0]
    dp_count = lax.axis_size("dp")
    text_span = text_rows * dp_count
    temper = jnp.exp(log_scale[0])
    logit_shift = logit_bias[0]
    partial_value = jnp.dot(features, proj_weight, preferred_element_type=jnp.float32)
    raw_embed = lax.psum(partial_value, "tp")
    image_inverse = lax.rsqrt(jnp.sum(raw_embed * raw_embed, axis=1, keepdims=True) + 1e-06)
    unit_full = raw_embed * image_inverse
    image_unit = unit_full.astype(jnp.bfloat16)
    text_value = text_embed.astype(jnp.float32)
    text_inverse = lax.rsqrt(jnp.sum(text_value * text_value, axis=1, keepdims=True) + 1e-06)
    text_full = text_value * text_inverse
    text_unit = text_full.astype(jnp.bfloat16)
    first_image = lax.axis_index("dp") * image_rows
    first_text = lax.axis_index("tp") * text_span
    image_ids = first_image + jnp.arange(image_rows, dtype=jnp.int32)[:, None]
    text_whole = lax.all_gather(text_unit, "dp", axis=0, tiled=True)
    logits = (
        temper
        * lax.dot_general(
            image_unit, text_whole, (((1,), (1,)), ((), ())), preferred_element_type=jnp.float32
        )
        + logit_shift
    )
    text_ids = first_text + jnp.arange(text_whole.shape[0], dtype=jnp.int32)[None, :]
    labels = jnp.where(image_ids == text_ids, 1.0, -1.0).astype(jnp.float32)
    coeffs = (-labels * jax.nn.sigmoid(-labels * logits) * temper).astype(jnp.bfloat16)
    grad_accum = jnp.dot(coeffs, text_whole, preferred_element_type=jnp.float32)
    coeff_table = coeffs
    unit_grad, coeff_table = (grad_accum, coeff_table)
    text_unit_grad = lax.psum_scatter(
        lax.dot_general(
            coeff_table, image_unit, (((0,), (0,)), ((), ())), preferred_element_type=jnp.float32
        ),
        "dp",
        scatter_dimension=0,
        tiled=True,
    )
    summed = lax.psum(unit_grad, "tp")
    embed_grad = unit_backward(summed, unit_full, image_inverse).astype(jnp.bfloat16)
    image_grad = lax.dot_general(
        embed_grad, proj_weight, (((1,), (1,)), ((), ())), preferred_element_type=jnp.float32
    ).astype(jnp.bfloat16)
    weight_part = lax.dot_general(
        features, embed_grad, (((0,), (0,)), ((), ())), preferred_element_type=jnp.float32
    )
    weight_grad = lax.psum(weight_part, "dp").astype(jnp.bfloat16)
    text_grad = unit_backward(text_unit_grad, text_full, text_inverse).astype(jnp.bfloat16)
    return (image_grad, weight_grad, text_grad)


def solution(mesh):
    return jax.shard_map(
        shards,
        mesh=mesh,
        in_specs=(P("dp", "tp"), P("tp", None), P(("tp", "dp"), None), P(), P()),
        out_specs=(P("dp", "tp"), P("tp", None), P(("tp", "dp"), None)),
        check_vma=False,
    )
```

profile of v0, /device:TPU:1, one launch (start us, length us, event | category | flops | bytes accessed | tf_op | source)
XLA Modules:
  0.0 761.7 jit_solution(13843336125627197882)
XLA Ops:
  8.0 0.0 all-reduce.4.cloned.1.call-start
  8.1 0.9 copy-done
  9.0 1.9 fusion.18
  10.9 0.0 all-gather.2.cloned.1.call-start
  10.9 0.9 fusion.16
  11.8 1.5 fusion.11
  13.3 0.0 all-gather.2.cloned.1.call-update
  13.3 0.0 all-reduce.6.cloned.1.call-start
  14.7 154.0 %all-reduce.4.cloned.1.call-done = f32[128,1024]{1,0:T(8,128)} async-done(((f32[128,1024]{1,0:T(8,128)}), f32[128,1024]{1,0:T(8,128)}) %all-reduce.4.cloned.1.call-update) | async-done | bytes 524304 | tf_op jit(solution)/shard_map/psum | solution.py:20
  168.7 1.2 multiply_reduce_fusion.1
  169.9 0.0 all-gather.2.cloned.1.call-done
  170.0 2.9 fusion.8
  172.9 1.3 fusion.19
  174.2 0.0 reduce-scatter.2.cloned.1.call-start
  174.2 2.7 fusion.17
  176.9 0.0 reduce-scatter.2.cloned.1.call-update
  176.9 148.0 %all-reduce.6.cloned.1.call-done = f32[128,1024]{1,0:T(8,128)} async-done(((f32[128,1024]{1,0:T(8,128)}), f32[128,1024]{1,0:T(8,128)}) %all-reduce.6.cloned.1.call-update) | async-done | bytes 524304 | tf_op jit(solution)/shard_map/psum | solution.py:53
  324.9 1.2 multiply_reduce_fusion
  326.1 1.2 multiply_convert_fusion
  327.4 0.2 convolution_bitcast_fusion
  327.6 0.9 convolution_convert_fusion
  328.5 423.2 %all-reduce.7 = bf16[192,1024]{1,0:T(8,128)(2,1)} all-reduce(f32[192,1024]{1,0:T(8,128)S(1)} %convolution_bitcast_fusion), channel_id=1, replica_groups=mesh['tp'=8,'dp'=64] {'dp'}, use_global_device_ids=true, to_apply=%region_5.6 | all-reduce | flops 196608 | bytes 1179648 | tf_op jit(solution)/shard_map/psum | solution.py:61
  751.7 1.0 fusion.12
  752.7 1.5 fusion.15
  (16 shorter events, 0.1 us)
Async XLA Ops:
  8.0 1.0 copy-start
  8.0 160.7 %all-reduce.4.cloned.1.call-start = ((), (), s32[]{:S(2)}) async-start(), calls=%async_computation.1 | async-start | bytes 1048576 | tf_op jit(solution)/shard_map/psum | solution.py:20
  10.9 159.1 %all-gather.2.cloned.1.call-start = ((), (), s32[]{:S(2)}) async-start(), calls=%async_computation.2 | async-start | bytes 2129920 | tf_op jit(solution)/shard_map/all_gather | solution.py:31
  13.3 311.6 %all-reduce.6.cloned.1.call-start = ((), (), s32[]{:S(2)}) async-start(), calls=%async_computation.3 | async-start | bytes 1048576 | tf_op jit(solution)/shard_map/psum | solution.py:53
  169.9 2.9 copy-start.2
  172.8 1.4 copy-start.1
  174.2 577.5 %reduce-scatter.2.cloned.1.call-start = ((), (), s32[]{:S(2)}) async-start(), calls=%async_computation.4 | async-start | bytes 4259840 | tf_op jit(solution)/shard_map/reduce_scatter | solution.py:45
  176.9 150.4 %copy-start.4 = (bf16[128,192]{0,1:T(8,128)(2,1)S(1)}, bf16[128,192]{0,1:T(8,128)(2,1)}, u32[]{:S(2)}) copy-start(bf16[128,192]{0,1:T(8,128)(2,1)} %param.5) | copy-start | bytes 147460
  326.1 425.6 %copy-start.3 = (bf16[16,1024]{1,0:T(8,128)(2,1)S(1)}, bf16[16,1024]{1,0:T(8,128)(2,1)}, u32[]{:S(2)}) copy-start(bf16[16,1024]{1,0:T(8,128)(2,1)} %param.7) | copy-start | bytes 98308
Sparse Core Ops, SparseCore 0:
  11.8 156.9 all-reduce.3
  174.3 150.5 all-reduce.5
Sparse Core Ops, SparseCore 1:
  14.3 132.4 all-gather.1
  177.4 435.1 reduce-scatter.1
where the time goes:
time: 768 us; the launch traced here: 762 us
  blocking collectives  423 us (55%)
  waiting for transfers between devices  302 us (39%)
  between operations  16.9 us (2%)
  matrix products  9.83 us (1%)
  other arithmetic  8.52 us (1%)
    psum x1, blocking collectives, shards(): weight_grad = lax.psum(weight_part, 'dp').astype(jnp.bfloat16)  423 us
    psum x1, waiting for transfers between devices, shards(): raw_embed = lax.psum(partial_value, 'tp')  154 us
    psum x1, waiting for transfers between devices, shards(): summed = lax.psum(unit_grad, 'tp')  148 us
  transfers between devices with their start and end apart: 4, of which 2 were waited for; matrix products, arithmetic and copies ran while one was open for 1% of the time, Pallas kernels for 0%

commit v1 on v0

v1 whole, which is shorter than its diff:
```python
import jax
import jax.numpy as jnp
from jax import lax
from jax.sharding import Mesh, PartitionSpec as P

AXES = ("zh", "x", "y", "zl", "c")
BF = jnp.bfloat16
F32 = jnp.float32


def exchange(value, axes):
    return lax.all_to_all(value, axes, 0, 0, tiled=False)


def gather(value, axes):
    count = lax.axis_size(axes)
    return exchange(jnp.broadcast_to(value[None], (count,) + value.shape), axes)


def swap(value, axis):
    return lax.ppermute(value, axis, [(0, 1), (1, 0)])


def unit_backward(grad_unit, unit_value, inverse):
    along = jnp.sum(unit_value * grad_unit, axis=1, keepdims=True)
    return inverse * (grad_unit - along * unit_value)


def shards(features, proj_weight, text_embed, log_scale, logit_bias):
    zh, x, y, zl, c = (lax.axis_index(name) for name in AXES)
    nx, ny, nzl = (lax.axis_size(name) for name in ("x", "y", "zl"))
    emb = proj_weight.shape[1]
    block_rows = features.shape[0]
    own_rows = block_rows // nx
    text_rows = text_embed.shape[0]
    temper = jnp.exp(log_scale[0])
    logit_shift = logit_bias[0]

    partial_value = jnp.dot(features, proj_weight, preferred_element_type=F32).astype(BF)
    parts = exchange(partial_value.reshape(nx, own_rows, emb), "x")
    half_embed = jnp.sum(parts.astype(F32), axis=0)

    text_value = text_embed.astype(F32)
    text_inverse = lax.rsqrt(jnp.sum(text_value * text_value, axis=1, keepdims=True) + 1e-06)
    text_full = text_value * text_inverse
    text_unit = text_full.astype(BF)

    half_sent, text_unit = lax.optimization_barrier((half_embed.astype(BF), text_unit))
    other_half = swap(half_sent, "zh")
    text_line = gather(text_unit, "zl").reshape(nzl * text_rows, emb)
    raw_embed = half_embed + other_half.astype(F32)
    text_pair = swap(text_line, "c")
    text_block = jnp.concatenate([text_line, text_pair], axis=0)

    image_inverse = lax.rsqrt(jnp.sum(raw_embed * raw_embed, axis=1, keepdims=True) + 1e-06)
    unit_full = raw_embed * image_inverse
    image_unit = unit_full.astype(BF)
    image_block = gather(image_unit, ("y", "x")).reshape(ny * block_rows, emb)

    image_y = jnp.arange(ny, dtype=jnp.int32)[:, None]
    image_r = jnp.arange(block_rows, dtype=jnp.int32)[None, :]
    image_ids = (((image_y * nzl + zl) * 2 + c) * block_rows + image_r).reshape(-1, 1)
    text_c = jnp.stack([c, 1 - c]).astype(jnp.int32)[:, None, None]
    text_l = jnp.arange(nzl, dtype=jnp.int32)[None, :, None]
    text_r = jnp.arange(text_rows, dtype=jnp.int32)[None, None, :]
    text_group = (zh * nx + x) * ny + y
    text_ids = (((text_group * nzl + text_l) * 2 + text_c) * text_rows + text_r).reshape(1, -1)

    logits = (
        temper
        * lax.dot_general(
            image_block, text_block, (((1,), (1,)), ((), ())), preferred_element_type=F32
        )
        + logit_shift
    )
    labels = jnp.where(image_ids == text_ids, 1.0, -1.0).astype(F32)
    coeffs = (-labels * jax.nn.sigmoid(-labels * logits) * temper).astype(BF)

    unit_part = jnp.dot(coeffs, text_block, preferred_element_type=F32).astype(BF)
    unit_parts = exchange(unit_part.reshape(ny * nx, own_rows, emb), ("y", "x"))
    half_grad = jnp.sum(unit_parts.astype(F32), axis=0)

    text_part = lax.dot_general(
        coeffs, image_block, (((0,), (0,)), ((), ())), preferred_element_type=F32
    )
    line_rows = nzl * text_rows
    text_away = swap(text_part[line_rows:].astype(BF), "c")
    text_home = (text_part[:line_rows] + text_away.astype(F32)).astype(BF)

    grad_sent, text_home = lax.optimization_barrier((half_grad.astype(BF), text_home))
    other_grad = swap(grad_sent, "zh")
    text_parts = exchange(text_home.reshape(nzl, text_rows, emb), "zl")
    unit_grad = half_grad + other_grad.astype(F32)
    embed_rows = unit_backward(unit_grad, unit_full, image_inverse).astype(BF)
    embed_grad = gather(embed_rows, "x").reshape(block_rows, emb)

    weight_part = lax.dot_general(
        features, embed_grad, (((0,), (0,)), ((), ())), preferred_element_type=F32
    ).astype(BF)
    image_grad = lax.dot_general(
        embed_grad, proj_weight, (((1,), (1,)), ((), ())), preferred_element_type=F32
    ).astype(BF)
    pieces = ny * 2
    weight_rows = weight_part.shape[0] // pieces
    weight_parts = exchange(weight_part.reshape(pieces, weight_rows, emb), ("y", "c"))
    weight_sum = jnp.sum(weight_parts.astype(F32), axis=0).astype(BF)
    weight_line = gather(weight_sum, "zl")
    weight_own = jnp.sum(weight_line.astype(F32), axis=0).astype(BF)
    weight_grad = gather(weight_own, ("y", "c")).reshape(weight_part.shape)

    text_unit_grad = jnp.sum(text_parts.astype(F32), axis=0)
    text_grad = unit_backward(text_unit_grad, text_full, text_inverse).astype(BF)
    return (image_grad, weight_grad, text_grad)


def solution(mesh):
    fine = Mesh(mesh.devices.reshape(2, 4, 4, 8, 2), AXES)
    tp, dp = ("zh", "x"), ("y", "zl", "c")
    return jax.shard_map(
        shards,
        mesh=fine,
        in_specs=(P(dp, tp), P(tp, None), P(tp + dp, None), P(), P()),
        out_specs=(P(dp, tp), P(tp, None), P(tp + dp, None)),
        check_vma=False,
    )
```

time: 768 us -> 198 us (0.26)
  blocking collectives: 423 us -> 27.8 us
  waiting for transfers between devices: 302 us -> 56.7 us
  starting transfers between devices: 0.17 us -> 96.7 us
  between operations: 16.9 us -> 2.17 us
    psum x1 -> x0, blocking collectives: 423 us -> none  [shards(): weight_grad = lax.psum(weight_part, 'dp').astype(jnp.bfloat16)]
    psum x2 -> x0, waiting for transfers between devices: 302 us -> none  [the longest x1 154 us: shards(): raw_embed = lax.psum(partial_value, 'tp')]
    all_to_all x0 -> x7, starting transfers between devices: none -> 63 us  [exchange(): return lax.all_to_all(value, axes, 0, 0, tiled=False)]
    all_to_all x0 -> x7, waiting for transfers between devices: none -> 45.1 us  [exchange(): return lax.all_to_all(value, axes, 0, 0, tiled=False)]
    ppermute x0 -> x4, starting transfers between devices: none -> 33.6 us  [swap(): return lax.ppermute(value, axis, [(0, 1), (1, 0)])]
    all_to_all x0 -> x2, blocking collectives: none -> 27.8 us  [exchange(): return lax.all_to_all(value, axes, 0, 0, tiled=False)]
    ppermute x0 -> x4, waiting for transfers between devices: none -> 11.7 us  [swap(): return lax.ppermute(value, axis, [(0, 1), (1, 0)])]
  transfers between devices with their start and end apart: 4 -> 11, of which waited for: 2 -> 9; matrix products, arithmetic and copies ran while one was open for 1% -> 2% of each run, Pallas kernels for 0% -> 0%
where the time goes in v1:
time: 198 us; the launch traced here: 197 us
  starting transfers between devices  96.7 us (49%)
  waiting for transfers between devices  56.7 us (29%)
  blocking collectives  27.8 us (14%)
  matrix products  5.36 us (3%)
  local copies, waits for them, and re-layouts  5.3 us (3%)
  other arithmetic  3.07 us (2%)
  between operations  2.17 us (1%)
    all_to_all x7, starting transfers between devices, exchange(): return lax.all_to_all(value, axes, 0, 0, tiled=False)  63 us
    all_to_all x7, waiting for transfers between devices, exchange(): return lax.all_to_all(value, axes, 0, 0, tiled=False)  45.1 us
    ppermute x4, starting transfers between devices, swap(): return lax.ppermute(value, axis, [(0, 1), (1, 0)])  33.6 us
    all_to_all x2, blocking collectives, exchange(): return lax.all_to_all(value, axes, 0, 0, tiled=False)  27.8 us
    ppermute x4, waiting for transfers between devices, swap(): return lax.ppermute(value, axis, [(0, 1), (1, 0)])  11.7 us
  transfers between devices with their start and end apart: 11, of which 9 were waited for; matrix products, arithmetic and copies ran while one was open for 2% of the time, Pallas kernels for 0%

profile of v1, /device:TPU:1, one launch (start us, length us, event | category | flops | bytes accessed | tf_op | source)
XLA Modules:
  0.0 197.2 jit_solution(10643277397040455733)
XLA Ops:
  1.6 1.8 convolution_convert_fusion.2
  3.4 4.8 %all-to-all-start = ((bf16[4,32,1024]{2,1,0:T(8,128)(2,1)}), bf16[4,32,1024]{2,1,0:T(8,128)(2,1)S(1)}, u32[]{:S(2)}, u32[]{:S(2)}) async-start(bf16[4,32,1024]{2,1,0:T(8,128)(2,1)} %bitcast), calls=%async_computation | async-start | bytes 524288 | tf_op jit(solution)/shard_map/all_to_all | solution.py:12
  8.4 5.3 %all-to-all-done = bf16[4,32,1024]{2,1,0:T(8,128)(2,1)S(1)} async-done(((bf16[4,32,1024]{2,1,0:T(8,128)(2,1)}), bf16[4,32,1024]{2,1,0:T(8,128)(2,1)S(1)}, u32[]{:S(2)}, u32[]{:S(2)}) %all-to-all-start) | async-done | bytes 262176 | tf_op jit(solution)/shard_map/all_to_all | solution.py:12
  14.5 12.3 %all-to-all-start.2 = ((bf16[8,16,1024]{2,1,0:T(8,128)(2,1)}), bf16[8,16,1024]{2,1,0:T(8,128)(2,1)S(1)}, u32[]{:S(2)}, u32[]{:S(2)}) async-start(bf16[8,16,1024]{2,1,0:T(8,128)(2,1)} %broadcast_in_dim.21), calls=%async_computation.2 | async-start | bytes 524288 | tf_op jit(solution)/shard_map/all_to_all | solution.py:12
  26.8 7.9 %collective-permute-start = (bf16[32,1024]{1,0:T(8,128)(2,1)S(1)}, bf16[32,1024]{1,0:T(8,128)(2,1)S(1)}, u32[]{:S(2)}, u32[]{:S(2)}) collective-permute-start(bf16[32,1024]{1,0:T(8,128)(2,1)S(1)} %convert_element_type.67), channel_id=1, source_target_pairs={{0,256},{256,0},{1,257},{257,1},{2,258},{258,2},{3,259},{259,3},{4... | collective-permute-start | bytes 196616 | tf_op jit(solution)/shard_map/ppermute | solution.py:21
  34.8 5.9 %collective-permute-done = bf16[32,1024]{1,0:T(8,128)(2,1)S(1)} collective-permute-done((bf16[32,1024]{1,0:T(8,128)(2,1)S(1)}, bf16[32,1024]{1,0:T(8,128)(2,1)S(1)}, u32[]{:S(2)}, u32[]{:S(2)}) %collective-permute-start) | collective-permute-done | bytes 65568 | tf_op jit(solution)/shard_map/ppermute | solution.py:21
  42.0 4.9 %all-to-all-start.1 = ((bf16[16,32,1024]{2,1,0:T(8,128)(2,1)}), bf16[16,32,1024]{2,1,0:T(8,128)(2,1)S(1)}, u32[]{:S(2)}, u32[]{:S(2)}) async-start(bf16[16,32,1024]{2,1,0:T(8,128)(2,1)} %broadcast_in_dim.20), calls=%async_computation.1 | async-start | bytes 2097152 | tf_op jit(solution)/shard_map/all_to_all | solution.py:12
  47.1 8.4 %collective-permute-start.1 = (bf16[128,1024]{1,0:T(8,128)(2,1)S(1)}, bf16[128,1024]{1,0:T(8,128)(2,1)S(1)}, u32[]{:S(2)}, u32[]{:S(2)}) collective-permute-start(bf16[128,1024]{1,0:T(8,128)(2,1)S(1)} %bitcast.33), channel_id=1, source_target_pairs={{0,1},{1,0},{2,3},{3,2},{4,5},{5,4},{6,7},{7,6},{8,9},{9,8},{10,11... | collective-permute-start | bytes 786440 | tf_op jit(solution)/shard_map/ppermute | solution.py:21
  57.0 2.3 %all-to-all-done.1 = bf16[16,32,1024]{2,1,0:T(8,128)(2,1)S(1)} async-done(((bf16[16,32,1024]{2,1,0:T(8,128)(2,1)}), bf16[16,32,1024]{2,1,0:T(8,128)(2,1)S(1)}, u32[]{:S(2)}, u32[]{:S(2)}) %all-to-all-start.1) | async-done | bytes 1048608 | tf_op jit(solution)/shard_map/all_to_all | solution.py:12
  59.9 1.4 convolution_convert_fusion
  61.3 4.7 %all-to-all-start.3 = ((bf16[16,32,1024]{2,1,0:T(8,128)(2,1)}), bf16[16,32,1024]{2,1,0:T(8,128)(2,1)S(1)}, u32[]{:S(2)}, u32[]{:S(2)}) async-start(bf16[16,32,1024]{2,1,0:T(8,128)(2,1)} %bitcast.8), calls=%async_computation.3 | async-start | bytes 2097152 | tf_op jit(solution)/shard_map/all_to_all | solution.py:12
  66.5 8.3 %collective-permute-start.2 = (bf16[128,1024]{1,0:T(8,128)(2,1)S(1)}, bf16[128,1024]{1,0:T(8,128)(2,1)S(1)}, u32[]{:S(2)}, u32[]{:S(2)}) collective-permute-start(bf16[128,1024]{1,0:T(8,128)(2,1)S(1)} %slice.15), channel_id=1, source_target_pairs={{0,1},{1,0},{2,3},{3,2},{4,5},{5,4},{6,7},{7,6},{8,9},{9,8},{10,11... | collective-permute-start | bytes 786440 | tf_op jit(solution)/shard_map/ppermute | solution.py:21
  74.8 1.1 collective-permute-done.2
  76.7 1.9 all-to-all-done.3
  78.8 9.0 %collective-permute-start.3 = (bf16[32,1024]{1,0:T(8,128)(2,1)S(1)}, bf16[32,1024]{1,0:T(8,128)(2,1)S(1)}, u32[]{:S(2)}, u32[]{:S(2)}) collective-permute-start(bf16[32,1024]{1,0:T(8,128)(2,1)S(1)} %convert_element_type.75), channel_id=1, source_target_pairs={{0,256},{256,0},{1,257},{257,1},{2,258},{258,2},{3,259},{259,3},{4... | collective-permute-start | bytes 196616 | tf_op jit(solution)/shard_map/ppermute | solution.py:21
  87.8 4.7 %collective-permute-done.3 = bf16[32,1024]{1,0:T(8,128)(2,1)S(1)} collective-permute-done((bf16[32,1024]{1,0:T(8,128)(2,1)S(1)}, bf16[32,1024]{1,0:T(8,128)(2,1)S(1)}, u32[]{:S(2)}, u32[]{:S(2)}) %collective-permute-start.3) | collective-permute-done | bytes 65568 | tf_op jit(solution)/shard_map/ppermute | solution.py:21
  92.8 7.9 %all_to_all.45 = bf16[4,32,1024]{2,1,0:T(8,128)(2,1)S(1)} all-to-all(bf16[4,32,1024]{2,1,0:T(8,128)(2,1)S(1)} %broadcast_in_dim.22), channel_id=1, replica_groups=mesh['zh'=2,'x'=4,'y'=4,'zl'=8,'c'=2] {'x'}, dimensions={0} | all-to-all | bytes 524288 | tf_op jit(solution)/shard_map/all_to_all | solution.py:12
  101.0 19.9 %all_to_all.46 = bf16[8,24,1024]{2,1,0:T(8,128)(2,1)S(1)} all-to-all(bf16[8,24,1024]{2,1,0:T(8,128)(2,1)S(1)} %bitcast.32), channel_id=1, replica_groups=mesh['zh'=2,'x'=4,'y'=4,'zl'=8,'c'=2] {'y','c'}, dimensions={0} | all-to-all | bytes 786432 | tf_op jit(solution)/shard_map/all_to_all | solution.py:12
  120.9 17.0 %all-to-all-start.8 = ((bf16[8,16,1024]{2,1,0:T(8,128)(2,1)}), bf16[8,16,1024]{2,1,0:T(8,128)(2,1)S(1)}, u32[]{:S(2)}, u32[]{:S(2)}) async-start(bf16[8,16,1024]{2,1,0:T(8,128)(2,1)} %bitcast.13), calls=%async_computation.8 | async-start | bytes 524288 | tf_op jit(solution)/shard_map/all_to_all | solution.py:12
  138.0 12.0 %all-to-all-done.8 = bf16[8,16,1024]{2,1,0:T(8,128)(2,1)S(1)} async-done(((bf16[8,16,1024]{2,1,0:T(8,128)(2,1)}), bf16[8,16,1024]{2,1,0:T(8,128)(2,1)S(1)}, u32[]{:S(2)}, u32[]{:S(2)}) %all-to-all-start.8) | async-done | bytes 262176 | tf_op jit(solution)/shard_map/all_to_all | solution.py:12
  150.7 9.3 %all-to-all-start.6 = ((bf16[8,24,1024]{2,1,0:T(8,128)(2,1)}), bf16[8,24,1024]{2,1,0:T(8,128)(2,1)S(1)}, u32[]{:S(2)}, u32[]{:S(2)}) async-start(bf16[8,24,1024]{2,1,0:T(8,128)(2,1)} %broadcast_in_dim.23), calls=%async_computation.6 | async-start | bytes 786432 | tf_op jit(solution)/shard_map/all_to_all | solution.py:12
  161.0 16.4 %all-to-all-done.6 = bf16[8,24,1024]{2,1,0:T(8,128)(2,1)S(1)} async-done(((bf16[8,24,1024]{2,1,0:T(8,128)(2,1)}), bf16[8,24,1024]{2,1,0:T(8,128)(2,1)S(1)}, u32[]{:S(2)}, u32[]{:S(2)}) %all-to-all-start.6) | async-done | bytes 393248 | tf_op jit(solution)/shard_map/all_to_all | solution.py:12
  178.2 10.1 %all-to-all-start.7 = ((bf16[8,24,1024]{2,1,0:T(8,128)(2,1)}), bf16[8,24,1024]{2,1,0:T(8,128)(2,1)S(1)}, u32[]{:S(2)}, u32[]{:S(2)}) async-start(bf16[8,24,1024]{2,1,0:T(8,128)(2,1)} %broadcast_in_dim.24), calls=%async_computation.7 | async-start | bytes 786432 | tf_op jit(solution)/shard_map/all_to_all | solution.py:12
  189.2 7.2 %all-to-all-done.7 = bf16[8,24,1024]{2,1,0:T(8,128)(2,1)S(1)} async-done(((bf16[8,24,1024]{2,1,0:T(8,128)(2,1)}), bf16[8,24,1024]{2,1,0:T(8,128)(2,1)S(1)}, u32[]{:S(2)}, u32[]{:S(2)}) %all-to-all-start.7) | async-done | bytes 393248 | tf_op jit(solution)/shard_map/all_to_all | solution.py:12
  (44 shorter events, 10.5 us)
Async XLA Ops:
  0.6 1.0 copy-start
  0.6 7.6 %copy-start.1 = (bf16[16,1024]{1,0:T(8,128)(2,1)S(1)}, bf16[16,1024]{1,0:T(8,128)(2,1)}, u32[]{:S(2)}) copy-start(bf16[16,1024]{1,0:T(8,128)(2,1)} %param.7) | copy-start | bytes 98308
  3.4 10.4 %all-to-all-start = ((bf16[4,32,1024]{2,1,0:T(8,128)(2,1)}), bf16[4,32,1024]{2,1,0:T(8,128)(2,1)S(1)}, u32[]{:S(2)}, u32[]{:S(2)}) async-start(bf16[4,32,1024]{2,1,0:T(8,128)(2,1)} %bitcast), calls=%async_computation | async-start | bytes 524288 | tf_op jit(solution)/shard_map/all_to_all | solution.py:12
  14.5 26.3 %all-to-all-start.2 = ((bf16[8,16,1024]{2,1,0:T(8,128)(2,1)}), bf16[8,16,1024]{2,1,0:T(8,128)(2,1)S(1)}, u32[]{:S(2)}, u32[]{:S(2)}) async-start(bf16[8,16,1024]{2,1,0:T(8,128)(2,1)} %broadcast_in_dim.21), calls=%async_computation.2 | async-start | bytes 524288 | tf_op jit(solution)/shard_map/all_to_all | solution.py:12
  26.8 13.8 %collective-permute-start = (bf16[32,1024]{1,0:T(8,128)(2,1)S(1)}, bf16[32,1024]{1,0:T(8,128)(2,1)S(1)}, u32[]{:S(2)}, u32[]{:S(2)}) collective-permute-start(bf16[32,1024]{1,0:T(8,128)(2,1)S(1)} %convert_element_type.67), channel_id=1, source_target_pairs={{0,256},{256,0},{1,257},{257,1},{2,258},{258,2},{3,259},{259,3},{4... | collective-permute-start | bytes 196616 | tf_op jit(solution)/shard_map/ppermute | solution.py:21
  42.0 17.3 %all-to-all-start.1 = ((bf16[16,32,1024]{2,1,0:T(8,128)(2,1)}), bf16[16,32,1024]{2,1,0:T(8,128)(2,1)S(1)}, u32[]{:S(2)}, u32[]{:S(2)}) async-start(bf16[16,32,1024]{2,1,0:T(8,128)(2,1)} %broadcast_in_dim.20), calls=%async_computation.1 | async-start | bytes 2097152 | tf_op jit(solution)/shard_map/all_to_all | solution.py:12
  47.1 12.2 %collective-permute-start.1 = (bf16[128,1024]{1,0:T(8,128)(2,1)S(1)}, bf16[128,1024]{1,0:T(8,128)(2,1)S(1)}, u32[]{:S(2)}, u32[]{:S(2)}) collective-permute-start(bf16[128,1024]{1,0:T(8,128)(2,1)S(1)} %bitcast.33), channel_id=1, source_target_pairs={{0,1},{1,0},{2,3},{3,2},{4,5},{5,4},{6,7},{7,6},{8,9},{9,8},{10,11... | collective-permute-start | bytes 786440 | tf_op jit(solution)/shard_map/ppermute | solution.py:21
  61.3 17.2 %all-to-all-start.3 = ((bf16[16,32,1024]{2,1,0:T(8,128)(2,1)}), bf16[16,32,1024]{2,1,0:T(8,128)(2,1)S(1)}, u32[]{:S(2)}, u32[]{:S(2)}) async-start(bf16[16,32,1024]{2,1,0:T(8,128)(2,1)} %bitcast.8), calls=%async_computation.3 | async-start | bytes 2097152 | tf_op jit(solution)/shard_map/all_to_all | solution.py:12
  66.5 9.4 %collective-permute-start.2 = (bf16[128,1024]{1,0:T(8,128)(2,1)S(1)}, bf16[128,1024]{1,0:T(8,128)(2,1)S(1)}, u32[]{:S(2)}, u32[]{:S(2)}) collective-permute-start(bf16[128,1024]{1,0:T(8,128)(2,1)S(1)} %slice.15), channel_id=1, source_target_pairs={{0,1},{1,0},{2,3},{3,2},{4,5},{5,4},{6,7},{7,6},{8,9},{9,8},{10,11... | collective-permute-start | bytes 786440 | tf_op jit(solution)/shard_map/ppermute | solution.py:21
  78.7 22.0 %copy-start.2 = (bf16[128,192]{0,1:T(8,128)(2,1)S(1)}, bf16[128,192]{0,1:T(8,128)(2,1)}, u32[]{:S(2)}) copy-start(bf16[128,192]{0,1:T(8,128)(2,1)} %param.5) | copy-start | bytes 147460
  78.8 13.7 %collective-permute-start.3 = (bf16[32,1024]{1,0:T(8,128)(2,1)S(1)}, bf16[32,1024]{1,0:T(8,128)(2,1)S(1)}, u32[]{:S(2)}, u32[]{:S(2)}) collective-permute-start(bf16[32,1024]{1,0:T(8,128)(2,1)S(1)} %convert_element_type.75), channel_id=1, source_target_pairs={{0,256},{256,0},{1,257},{257,1},{2,258},{258,2},{3,259},{259,3},{4... | collective-permute-start | bytes 196616 | tf_op jit(solution)/shard_map/ppermute | solution.py:21
  120.9 29.1 %all-to-all-start.8 = ((bf16[8,16,1024]{2,1,0:T(8,128)(2,1)}), bf16[8,16,1024]{2,1,0:T(8,128)(2,1)S(1)}, u32[]{:S(2)}, u32[]{:S(2)}) async-start(bf16[8,16,1024]{2,1,0:T(8,128)(2,1)} %bitcast.13), calls=%async_computation.8 | async-start | bytes 524288 | tf_op jit(solution)/shard_map/all_to_all | solution.py:12
  150.7 26.6 %all-to-all-start.6 = ((bf16[8,24,1024]{2,1,0:T(8,128)(2,1)}), bf16[8,24,1024]{2,1,0:T(8,128)(2,1)S(1)}, u32[]{:S(2)}, u32[]{:S(2)}) async-start(bf16[8,24,1024]{2,1,0:T(8,128)(2,1)} %broadcast_in_dim.23), calls=%async_computation.6 | async-start | bytes 786432 | tf_op jit(solution)/shard_map/all_to_all | solution.py:12
  178.2 18.2 %all-to-all-start.7 = ((bf16[8,24,1024]{2,1,0:T(8,128)(2,1)}), bf16[8,24,1024]{2,1,0:T(8,128)(2,1)S(1)}, u32[]{:S(2)}, u32[]{:S(2)}) async-start(bf16[8,24,1024]{2,1,0:T(8,128)(2,1)} %broadcast_in_dim.24), calls=%async_computation.7 | async-start | bytes 786432 | tf_op jit(solution)/shard_map/all_to_all | solution.py:12

commit v2 on v1

--- a/solution.py
+++ b/solution.py
@@ -17,8 +17,8 @@
     return exchange(jnp.broadcast_to(value[None], (count,) + value.shape), axes)
 
 
-def swap(value, axis):
-    return lax.ppermute(value, axis, [(0, 1), (1, 0)])
+def flip(value, axis, bit=1):
+    return lax.ppermute(value, axis, [(i, i ^ bit) for i in range(lax.axis_size(axis))])
 
 
 def unit_backward(grad_unit, unit_value, inverse):
@@ -46,10 +46,10 @@
     text_unit = text_full.astype(BF)
 
     half_sent, text_unit = lax.optimization_barrier((half_embed.astype(BF), text_unit))
-    other_half = swap(half_sent, "zh")
+    other_half = flip(half_sent, "zh")
     text_line = gather(text_unit, "zl").reshape(nzl * text_rows, emb)
     raw_embed = half_embed + other_half.astype(F32)
-    text_pair = swap(text_line, "c")
+    text_pair = flip(text_line, "c")
     text_block = jnp.concatenate([text_line, text_pair], axis=0)
 
     image_inverse = lax.rsqrt(jnp.sum(raw_embed * raw_embed, axis=1, keepdims=True) + 1e-06)
@@ -78,18 +78,17 @@
 
     unit_part = jnp.dot(coeffs, text_block, preferred_element_type=F32).astype(BF)
     unit_parts = exchange(unit_part.reshape(ny * nx, own_rows, emb), ("y", "x"))
-    half_grad = jnp.sum(unit_parts.astype(F32), axis=0)
 
     text_part = lax.dot_general(
         coeffs, image_block, (((0,), (0,)), ((), ())), preferred_element_type=F32
     )
     line_rows = nzl * text_rows
-    text_away = swap(text_part[line_rows:].astype(BF), "c")
+    text_away = flip(text_part[line_rows:].astype(BF), "c")
     text_home = (text_part[:line_rows] + text_away.astype(F32)).astype(BF)
 
-    grad_sent, text_home = lax.optimization_barrier((half_grad.astype(BF), text_home))
-    other_grad = swap(grad_sent, "zh")
-    text_parts = exchange(text_home.reshape(nzl, text_rows, emb), "zl")
+    unit_parts, text_home = lax.optimization_barrier((unit_parts, text_home))
+    half_grad = jnp.sum(unit_parts.astype(F32), axis=0)
+    other_grad = flip(half_grad.astype(BF), "zh")
     unit_grad = half_grad + other_grad.astype(F32)
     embed_rows = unit_backward(unit_grad, unit_full, image_inverse).astype(BF)
     embed_grad = gather(embed_rows, "x").reshape(block_rows, emb)
@@ -104,11 +103,19 @@
     weight_rows = weight_part.shape[0] // pieces
     weight_parts = exchange(weight_part.reshape(pieces, weight_rows, emb), ("y", "c"))
     weight_sum = jnp.sum(weight_parts.astype(F32), axis=0).astype(BF)
-    weight_line = gather(weight_sum, "zl")
-    weight_own = jnp.sum(weight_line.astype(F32), axis=0).astype(BF)
-    weight_grad = gather(weight_own, ("y", "c")).reshape(weight_part.shape)
+    text_sum = text_home.astype(F32).reshape(2, 2, 2, text_rows, emb)
+    for bit, depth in ((1, 2), (2, 1), (4, 0)):
+        upper = (zl & bit) > 0
+        first = lax.index_in_dim(text_sum, 0, depth, keepdims=False)
+        second = lax.index_in_dim(text_sum, 1, depth, keepdims=False)
+        away = jnp.where(upper, first, second).astype(BF)
+        sent = jnp.concatenate([weight_sum, away.reshape(-1, emb)], axis=0)
+        came = flip(sent, "zl", bit).astype(F32)
+        weight_sum = (weight_sum.astype(F32) + came[:weight_rows]).astype(BF)
+        text_sum = jnp.where(upper, second, first) + came[weight_rows:].reshape(away.shape)
+    text_unit_grad = text_sum
+    weight_grad = gather(weight_sum, ("y", "c")).reshape(weight_part.shape)
 
-    text_unit_grad = jnp.sum(text_parts.astype(F32), axis=0)
     text_grad = unit_backward(text_unit_grad, text_full, text_inverse).astype(BF)
     return (image_grad, weight_grad, text_grad)
 

time: 198 us -> 179 us (0.904)
  blocking collectives: 27.8 us -> 0 us
  starting transfers between devices: 96.7 us -> 105 us
    all_to_all x2 -> x0, blocking collectives: 27.8 us -> none  [exchange(): return lax.all_to_all(value, axes, 0, 0, tiled=False)]
    ppermute x4 -> x7, starting transfers between devices: 33.6 us -> 57.9 us  [flip(): lax.ppermute(value, axis, [(i, i ^ bit) for i in range(lax.axis_size(axis...]
    all_to_all x7, starting transfers between devices: 63 us -> 46.7 us  [exchange(): return lax.all_to_all(value, axes, 0, 0, tiled=False)]
    ppermute x4 -> x7, waiting for transfers between devices: 11.7 us -> 26.4 us  [flip(): lax.ppermute(value, axis, [(i, i ^ bit) for i in range(lax.axis_size(axis...]
    all_to_all x7, waiting for transfers between devices: 45.1 us -> 30.8 us  [exchange(): return lax.all_to_all(value, axes, 0, 0, tiled=False)]
  transfers between devices with their start and end apart: 11 -> 14, of which waited for: 9 -> 12; matrix products, arithmetic and copies ran while one was open for 2% -> 2% of each run, Pallas kernels for 0% -> 0%
where the time goes in v2:
time: 179 us; the launch traced here: 178 us
  starting transfers between devices  105 us (59%)
  waiting for transfers between devices  57.2 us (32%)
  matrix products  6.1 us (3%)
  local copies, waits for them, and re-layouts  5.28 us (3%)
  other arithmetic  2.54 us (1%)
  between operations  2.31 us (1%)
    ppermute x7, starting transfers between devices, flip(): lax.ppermute(value, axis, [(i, i ^ bit) for i in range(lax.axis_size(axis...  57.9 us
    all_to_all x7, starting transfers between devices, exchange(): return lax.all_to_all(value, axes, 0, 0, tiled=False)  46.7 us
    all_to_all x7, waiting for transfers between devices, exchange(): return lax.all_to_all(value, axes, 0, 0, tiled=False)  30.8 us
    ppermute x7, waiting for transfers between devices, flip(): lax.ppermute(value, axis, [(i, i ^ bit) for i in range(lax.axis_size(axis...  26.4 us
  transfers between devices with their start and end apart: 14, of which 12 were waited for; matrix products, arithmetic and copies ran while one was open for 2% of the time, Pallas kernels for 0%

profile of v2, /device:TPU:1, one launch (start us, length us, event | category | flops | bytes accessed | tf_op | source)
XLA Modules:
  0.0 178.1 jit_solution(11440016426135369553)
XLA Ops:
  3.4 4.8 %all-to-all-start = ((bf16[4,32,1024]{2,1,0:T(8,128)(2,1)}), bf16[4,32,1024]{2,1,0:T(8,128)(2,1)S(1)}, u32[]{:S(2)}, u32[]{:S(2)}) async-start(bf16[4,32,1024]{2,1,0:T(8,128)(2,1)} %bitcast), calls=%async_computation | async-start | bytes 524288 | tf_op jit(solution)/shard_map/all_to_all | solution.py:12
  8.4 5.3 %all-to-all-done = bf16[4,32,1024]{2,1,0:T(8,128)(2,1)S(1)} async-done(((bf16[4,32,1024]{2,1,0:T(8,128)(2,1)}), bf16[4,32,1024]{2,1,0:T(8,128)(2,1)S(1)}, u32[]{:S(2)}, u32[]{:S(2)}) %all-to-all-start) | async-done | bytes 262176 | tf_op jit(solution)/shard_map/all_to_all | solution.py:12
  14.5 12.3 %all-to-all-start.2 = ((bf16[8,16,1024]{2,1,0:T(8,128)(2,1)}), bf16[8,16,1024]{2,1,0:T(8,128)(2,1)S(1)}, u32[]{:S(2)}, u32[]{:S(2)}) async-start(bf16[8,16,1024]{2,1,0:T(8,128)(2,1)} %broadcast_in_dim.19), calls=%async_computation.2 | async-start | bytes 524288 | tf_op jit(solution)/shard_map/all_to_all | solution.py:12
  26.8 7.9 %collective-permute-start = (bf16[32,1024]{1,0:T(8,128)(2,1)S(1)}, bf16[32,1024]{1,0:T(8,128)(2,1)S(1)}, u32[]{:S(2)}, u32[]{:S(2)}) collective-permute-start(bf16[32,1024]{1,0:T(8,128)(2,1)S(1)} %convert_element_type.110), channel_id=1, source_target_pairs={{0,256},{256,0},{1,257},{257,1},{2,258},{258,2},{3,259},{259,3},{4... | collective-permute-start | bytes 196616 | tf_op jit(solution)/shard_map/ppermute | solution.py:21
  34.8 5.9 %collective-permute-done = bf16[32,1024]{1,0:T(8,128)(2,1)S(1)} collective-permute-done((bf16[32,1024]{1,0:T(8,128)(2,1)S(1)}, bf16[32,1024]{1,0:T(8,128)(2,1)S(1)}, u32[]{:S(2)}, u32[]{:S(2)}) %collective-permute-start) | collective-permute-done | bytes 65568 | tf_op jit(solution)/shard_map/ppermute | solution.py:21
  42.0 4.9 %all-to-all-start.1 = ((bf16[16,32,1024]{2,1,0:T(8,128)(2,1)}), bf16[16,32,1024]{2,1,0:T(8,128)(2,1)S(1)}, u32[]{:S(2)}, u32[]{:S(2)}) async-start(bf16[16,32,1024]{2,1,0:T(8,128)(2,1)} %broadcast_in_dim.16), calls=%async_computation.1 | async-start | bytes 2097152 | tf_op jit(solution)/shard_map/all_to_all | solution.py:12
  47.1 8.4 %collective-permute-start.1 = (bf16[128,1024]{1,0:T(8,128)(2,1)S(1)}, bf16[128,1024]{1,0:T(8,128)(2,1)S(1)}, u32[]{:S(2)}, u32[]{:S(2)}) collective-permute-start(bf16[128,1024]{1,0:T(8,128)(2,1)S(1)} %bitcast.47), channel_id=1, source_target_pairs={{0,1},{1,0},{2,3},{3,2},{4,5},{5,4},{6,7},{7,6},{8,9},{9,8},{10,11... | collective-permute-start | bytes 786440 | tf_op jit(solution)/shard_map/ppermute | solution.py:21
  61.3 4.6 %all-to-all-start.3 = ((bf16[16,32,1024]{2,1,0:T(8,128)(2,1)}), bf16[16,32,1024]{2,1,0:T(8,128)(2,1)S(1)}, u32[]{:S(2)}, u32[]{:S(2)}) async-start(bf16[16,32,1024]{2,1,0:T(8,128)(2,1)} %bitcast.8), calls=%async_computation.3 | async-start | bytes 2097152 | tf_op jit(solution)/shard_map/all_to_all | solution.py:12
  66.4 8.3 %collective-permute-start.2 = (bf16[128,1024]{1,0:T(8,128)(2,1)S(1)}, bf16[128,1024]{1,0:T(8,128)(2,1)S(1)}, u32[]{:S(2)}, u32[]{:S(2)}) collective-permute-start(bf16[128,1024]{1,0:T(8,128)(2,1)S(1)} %slice.97), channel_id=1, source_target_pairs={{0,1},{1,0},{2,3},{3,2},{4,5},{5,4},{6,7},{7,6},{8,9},{9,8},{10,11... | collective-permute-start | bytes 786440 | tf_op jit(solution)/shard_map/ppermute | solution.py:21
  75.9 2.5 %all-to-all-done.3 = bf16[16,32,1024]{2,1,0:T(8,128)(2,1)S(1)} async-done(((bf16[16,32,1024]{2,1,0:T(8,128)(2,1)}), bf16[16,32,1024]{2,1,0:T(8,128)(2,1)S(1)}, u32[]{:S(2)}, u32[]{:S(2)}) %all-to-all-start.3) | async-done | bytes 1048608 | tf_op jit(solution)/shard_map/all_to_all | solution.py:12
  78.7 9.0 %collective-permute-start.3 = (bf16[32,1024]{1,0:T(8,128)(2,1)S(1)}, bf16[32,1024]{1,0:T(8,128)(2,1)S(1)}, u32[]{:S(2)}, u32[]{:S(2)}) collective-permute-start(bf16[32,1024]{1,0:T(8,128)(2,1)S(1)} %convert_element_type.120), channel_id=1, source_target_pairs={{0,256},{256,0},{1,257},{257,1},{2,258},{258,2},{3,259},{259,3},{4... | collective-permute-start | bytes 196616 | tf_op jit(solution)/shard_map/ppermute | solution.py:21
  87.8 4.7 %collective-permute-done.3 = bf16[32,1024]{1,0:T(8,128)(2,1)S(1)} collective-permute-done((bf16[32,1024]{1,0:T(8,128)(2,1)S(1)}, bf16[32,1024]{1,0:T(8,128)(2,1)S(1)}, u32[]{:S(2)}, u32[]{:S(2)}) %collective-permute-start.3) | collective-permute-done | bytes 65568 | tf_op jit(solution)/shard_map/ppermute | solution.py:21
  93.4 3.4 %all-to-all-start.4 = ((bf16[4,32,1024]{2,1,0:T(8,128)(2,1)}), bf16[4,32,1024]{2,1,0:T(8,128)(2,1)S(1)}, u32[]{:S(2)}, u32[]{:S(2)}) async-start(bf16[4,32,1024]{2,1,0:T(8,128)(2,1)} %broadcast_in_dim.20), calls=%async_computation.4 | async-start | bytes 524288 | tf_op jit(solution)/shard_map/all_to_all | solution.py:12
  96.9 5.5 %all-to-all-done.4 = bf16[4,32,1024]{2,1,0:T(8,128)(2,1)S(1)} async-done(((bf16[4,32,1024]{2,1,0:T(8,128)(2,1)}), bf16[4,32,1024]{2,1,0:T(8,128)(2,1)S(1)}, u32[]{:S(2)}, u32[]{:S(2)}) %all-to-all-start.4) | async-done | bytes 262176 | tf_op jit(solution)/shard_map/all_to_all | solution.py:12
  103.4 12.8 %all-to-all-start.5 = ((bf16[8,24,1024]{2,1,0:T(8,128)(2,1)}), bf16[8,24,1024]{2,1,0:T(8,128)(2,1)S(1)}, u32[]{:S(2)}, u32[]{:S(2)}) async-start(bf16[8,24,1024]{2,1,0:T(8,128)(2,1)} %bitcast.11), calls=%async_computation.5 | async-start | bytes 786432 | tf_op jit(solution)/shard_map/all_to_all | solution.py:12
  116.3 8.0 %all-to-all-done.5 = bf16[8,24,1024]{2,1,0:T(8,128)(2,1)S(1)} async-done(((bf16[8,24,1024]{2,1,0:T(8,128)(2,1)}), bf16[8,24,1024]{2,1,0:T(8,128)(2,1)S(1)}, u32[]{:S(2)}, u32[]{:S(2)}) %all-to-all-start.5) | async-done | bytes 393248 | tf_op jit(solution)/shard_map/all_to_all | solution.py:12
  124.4 6.6 %collective-permute-start.4 = (bf16[88,1024]{1,0:T(8,128)(2,1)S(1)}, bf16[88,1024]{1,0:T(8,128)(2,1)S(1)}, u32[]{:S(2)}, u32[]{:S(2)}) collective-permute-start(bf16[88,1024]{1,0:T(8,128)(2,1)S(1)} %pad_maximum_fusion.3), channel_id=1, source_target_pairs={{0,2},{2,0},{4,6},{6,4},{8,10},{10,8},{12,14},{14,12},{1,3},{3,1},... | collective-permute-start | bytes 540680 | tf_op jit(solution)/shard_map/ppermute | solution.py:21
  131.0 4.0 %collective-permute-done.4 = bf16[88,1024]{1,0:T(8,128)(2,1)S(1)} collective-permute-done((bf16[88,1024]{1,0:T(8,128)(2,1)S(1)}, bf16[88,1024]{1,0:T(8,128)(2,1)S(1)}, u32[]{:S(2)}, u32[]{:S(2)}) %collective-permute-start.4) | collective-permute-done | bytes 180256 | tf_op jit(solution)/shard_map/ppermute | solution.py:21
  135.2 9.5 %collective-permute-start.5 = (bf16[56,1024]{1,0:T(8,128)(2,1)S(1)}, bf16[56,1024]{1,0:T(8,128)(2,1)S(1)}, u32[]{:S(2)}, u32[]{:S(2)}) collective-permute-start(bf16[56,1024]{1,0:T(8,128)(2,1)S(1)} %pad_maximum_fusion.4), channel_id=1, source_target_pairs={{0,4},{2,6},{4,0},{6,2},{8,12},{10,14},{12,8},{14,10},{1,5},{3,7},... | collective-permute-start | bytes 344072 | tf_op jit(solution)/shard_map/ppermute | solution.py:21
  144.7 5.6 %collective-permute-done.5 = bf16[56,1024]{1,0:T(8,128)(2,1)S(1)} collective-permute-done((bf16[56,1024]{1,0:T(8,128)(2,1)S(1)}, bf16[56,1024]{1,0:T(8,128)(2,1)S(1)}, u32[]{:S(2)}, u32[]{:S(2)}) %collective-permute-start.5) | collective-permute-done | bytes 114720 | tf_op jit(solution)/shard_map/ppermute | solution.py:21
  150.5 8.1 %collective-permute-start.6 = (bf16[40,1024]{1,0:T(8,128)(2,1)S(1)}, bf16[40,1024]{1,0:T(8,128)(2,1)S(1)}, u32[]{:S(2)}, u32[]{:S(2)}) collective-permute-start(bf16[40,1024]{1,0:T(8,128)(2,1)S(1)} %pad_maximum_fusion.5), channel_id=1, source_target_pairs={{0,8},{2,10},{4,12},{6,14},{8,0},{10,2},{12,4},{14,6},{1,9},{3,11}... | collective-permute-start | bytes 245768 | tf_op jit(solution)/shard_map/ppermute | solution.py:21
  159.5 5.0 %collective-permute-done.6 = bf16[40,1024]{1,0:T(8,128)(2,1)S(1)} collective-permute-done((bf16[40,1024]{1,0:T(8,128)(2,1)S(1)}, bf16[40,1024]{1,0:T(8,128)(2,1)S(1)}, u32[]{:S(2)}, u32[]{:S(2)}) %collective-permute-start.6) | collective-permute-done | bytes 81952 | tf_op jit(solution)/shard_map/ppermute | solution.py:21
  165.4 3.8 %all-to-all-start.6 = ((bf16[8,24,1024]{2,1,0:T(8,128)(2,1)}), bf16[8,24,1024]{2,1,0:T(8,128)(2,1)S(1)}, u32[]{:S(2)}, u32[]{:S(2)}) async-start(bf16[8,24,1024]{2,1,0:T(8,128)(2,1)} %broadcast_in_dim.21), calls=%async_computation.6 | async-start | bytes 786432 | tf_op jit(solution)/shard_map/all_to_all | solution.py:12
  170.1 7.2 %all-to-all-done.6 = bf16[8,24,1024]{2,1,0:T(8,128)(2,1)S(1)} async-done(((bf16[8,24,1024]{2,1,0:T(8,128)(2,1)}), bf16[8,24,1024]{2,1,0:T(8,128)(2,1)S(1)}, u32[]{:S(2)}, u32[]{:S(2)}) %all-to-all-start.6) | async-done | bytes 393248 | tf_op jit(solution)/shard_map/all_to_all | solution.py:12
  (63 shorter events, 17.4 us)
Async XLA Ops:
  0.6 1.0 copy-start
  0.6 7.6 %copy-start.1 = (bf16[16,1024]{1,0:T(8,128)(2,1)S(1)}, bf16[16,1024]{1,0:T(8,128)(2,1)}, u32[]{:S(2)}) copy-start(bf16[16,1024]{1,0:T(8,128)(2,1)} %param.7) | copy-start | bytes 98308
  3.4 10.4 %all-to-all-start = ((bf16[4,32,1024]{2,1,0:T(8,128)(2,1)}), bf16[4,32,1024]{2,1,0:T(8,128)(2,1)S(1)}, u32[]{:S(2)}, u32[]{:S(2)}) async-start(bf16[4,32,1024]{2,1,0:T(8,128)(2,1)} %bitcast), calls=%async_computation | async-start | bytes 524288 | tf_op jit(solution)/shard_map/all_to_all | solution.py:12
  14.5 26.3 %all-to-all-start.2 = ((bf16[8,16,1024]{2,1,0:T(8,128)(2,1)}), bf16[8,16,1024]{2,1,0:T(8,128)(2,1)S(1)}, u32[]{:S(2)}, u32[]{:S(2)}) async-start(bf16[8,16,1024]{2,1,0:T(8,128)(2,1)} %broadcast_in_dim.19), calls=%async_computation.2 | async-start | bytes 524288 | tf_op jit(solution)/shard_map/all_to_all | solution.py:12
  26.8 13.8 %collective-permute-start = (bf16[32,1024]{1,0:T(8,128)(2,1)S(1)}, bf16[32,1024]{1,0:T(8,128)(2,1)S(1)}, u32[]{:S(2)}, u32[]{:S(2)}) collective-permute-start(bf16[32,1024]{1,0:T(8,128)(2,1)S(1)} %convert_element_type.110), channel_id=1, source_target_pairs={{0,256},{256,0},{1,257},{257,1},{2,258},{258,2},{3,259},{259,3},{4... | collective-permute-start | bytes 196616 | tf_op jit(solution)/shard_map/ppermute | solution.py:21
  42.0 17.3 %all-to-all-start.1 = ((bf16[16,32,1024]{2,1,0:T(8,128)(2,1)}), bf16[16,32,1024]{2,1,0:T(8,128)(2,1)S(1)}, u32[]{:S(2)}, u32[]{:S(2)}) async-start(bf16[16,32,1024]{2,1,0:T(8,128)(2,1)} %broadcast_in_dim.16), calls=%async_computation.1 | async-start | bytes 2097152 | tf_op jit(solution)/shard_map/all_to_all | solution.py:12
  47.1 12.2 %collective-permute-start.1 = (bf16[128,1024]{1,0:T(8,128)(2,1)S(1)}, bf16[128,1024]{1,0:T(8,128)(2,1)S(1)}, u32[]{:S(2)}, u32[]{:S(2)}) collective-permute-start(bf16[128,1024]{1,0:T(8,128)(2,1)S(1)} %bitcast.47), channel_id=1, source_target_pairs={{0,1},{1,0},{2,3},{3,2},{4,5},{5,4},{6,7},{7,6},{8,9},{9,8},{10,11... | collective-permute-start | bytes 786440 | tf_op jit(solution)/shard_map/ppermute | solution.py:21
  61.3 17.2 %all-to-all-start.3 = ((bf16[16,32,1024]{2,1,0:T(8,128)(2,1)}), bf16[16,32,1024]{2,1,0:T(8,128)(2,1)S(1)}, u32[]{:S(2)}, u32[]{:S(2)}) async-start(bf16[16,32,1024]{2,1,0:T(8,128)(2,1)} %bitcast.8), calls=%async_computation.3 | async-start | bytes 2097152 | tf_op jit(solution)/shard_map/all_to_all | solution.py:12
  66.4 9.5 %collective-permute-start.2 = (bf16[128,1024]{1,0:T(8,128)(2,1)S(1)}, bf16[128,1024]{1,0:T(8,128)(2,1)S(1)}, u32[]{:S(2)}, u32[]{:S(2)}) collective-permute-start(bf16[128,1024]{1,0:T(8,128)(2,1)S(1)} %slice.97), channel_id=1, source_target_pairs={{0,1},{1,0},{2,3},{3,2},{4,5},{5,4},{6,7},{7,6},{8,9},{9,8},{10,11... | collective-permute-start | bytes 786440 | tf_op jit(solution)/shard_map/ppermute | solution.py:21
  78.7 23.7 %copy-start.2 = (bf16[128,192]{0,1:T(8,128)(2,1)S(1)}, bf16[128,192]{0,1:T(8,128)(2,1)}, u32[]{:S(2)}) copy-start(bf16[128,192]{0,1:T(8,128)(2,1)} %param.5) | copy-start | bytes 147460
  78.7 13.7 %collective-permute-start.3 = (bf16[32,1024]{1,0:T(8,128)(2,1)S(1)}, bf16[32,1024]{1,0:T(8,128)(2,1)S(1)}, u32[]{:S(2)}, u32[]{:S(2)}) collective-permute-start(bf16[32,1024]{1,0:T(8,128)(2,1)S(1)} %convert_element_type.120), channel_id=1, source_target_pairs={{0,256},{256,0},{1,257},{257,1},{2,258},{258,2},{3,259},{259,3},{4... | collective-permute-start | bytes 196616 | tf_op jit(solution)/shard_map/ppermute | solution.py:21
  93.4 8.9 %all-to-all-start.4 = ((bf16[4,32,1024]{2,1,0:T(8,128)(2,1)}), bf16[4,32,1024]{2,1,0:T(8,128)(2,1)S(1)}, u32[]{:S(2)}, u32[]{:S(2)}) async-start(bf16[4,32,1024]{2,1,0:T(8,128)(2,1)} %broadcast_in_dim.20), calls=%async_computation.4 | async-start | bytes 524288 | tf_op jit(solution)/shard_map/all_to_all | solution.py:12
  103.4 20.9 %all-to-all-start.5 = ((bf16[8,24,1024]{2,1,0:T(8,128)(2,1)}), bf16[8,24,1024]{2,1,0:T(8,128)(2,1)S(1)}, u32[]{:S(2)}, u32[]{:S(2)}) async-start(bf16[8,24,1024]{2,1,0:T(8,128)(2,1)} %bitcast.11), calls=%async_computation.5 | async-start | bytes 786432 | tf_op jit(solution)/shard_map/all_to_all | solution.py:12
  124.4 10.7 %collective-permute-start.4 = (bf16[88,1024]{1,0:T(8,128)(2,1)S(1)}, bf16[88,1024]{1,0:T(8,128)(2,1)S(1)}, u32[]{:S(2)}, u32[]{:S(2)}) collective-permute-start(bf16[88,1024]{1,0:T(8,128)(2,1)S(1)} %pad_maximum_fusion.3), channel_id=1, source_target_pairs={{0,2},{2,0},{4,6},{6,4},{8,10},{10,8},{12,14},{14,12},{1,3},{3,1},... | collective-permute-start | bytes 540680 | tf_op jit(solution)/shard_map/ppermute | solution.py:21
  135.2 15.1 %collective-permute-start.5 = (bf16[56,1024]{1,0:T(8,128)(2,1)S(1)}, bf16[56,1024]{1,0:T(8,128)(2,1)S(1)}, u32[]{:S(2)}, u32[]{:S(2)}) collective-permute-start(bf16[56,1024]{1,0:T(8,128)(2,1)S(1)} %pad_maximum_fusion.4), channel_id=1, source_target_pairs={{0,4},{2,6},{4,0},{6,2},{8,12},{10,14},{12,8},{14,10},{1,5},{3,7},... | collective-permute-start | bytes 344072 | tf_op jit(solution)/shard_map/ppermute | solution.py:21
  150.5 14.1 %collective-permute-start.6 = (bf16[40,1024]{1,0:T(8,128)(2,1)S(1)}, bf16[40,1024]{1,0:T(8,128)(2,1)S(1)}, u32[]{:S(2)}, u32[]{:S(2)}) collective-permute-start(bf16[40,1024]{1,0:T(8,128)(2,1)S(1)} %pad_maximum_fusion.5), channel_id=1, source_target_pairs={{0,8},{2,10},{4,12},{6,14},{8,0},{10,2},{12,4},{14,6},{1,9},{3,11}... | collective-permute-start | bytes 245768 | tf_op jit(solution)/shard_map/ppermute | solution.py:21
  165.4 11.9 %all-to-all-start.6 = ((bf16[8,24,1024]{2,1,0:T(8,128)(2,1)}), bf16[8,24,1024]{2,1,0:T(8,128)(2,1)S(1)}, u32[]{:S(2)}, u32[]{:S(2)}) async-start(bf16[8,24,1024]{2,1,0:T(8,128)(2,1)} %broadcast_in_dim.21), calls=%async_computation.6 | async-start | bytes 786432 | tf_op jit(solution)/shard_map/all_to_all | solution.py:12

commit v3 on v1

v3 whole, which is shorter than its diff:
```python
import jax
import jax.numpy as jnp
from jax import lax
from jax.sharding import Mesh, PartitionSpec as P

AXES = ("zh", "x", "y", "zq", "zp", "c")
SIZES = (2, 4, 4, 4, 2, 2)
BF = jnp.bfloat16
F32 = jnp.float32


def exchange(value, axes):
    return lax.all_to_all(value, axes, 0, 0, tiled=False)


def gather(value, axes):
    count = lax.axis_size(axes)
    return exchange(jnp.broadcast_to(value[None], (count,) + value.shape), axes)


def flip(value, axis):
    return lax.ppermute(value, axis, [(0, 1), (1, 0)])


def fold(value, axis):
    rows = value.shape[0] // 2
    return value[:rows] + flip(value[rows:].astype(BF), axis).astype(F32)


def unit_backward(grad_unit, unit_value, inverse):
    along = jnp.sum(unit_value * grad_unit, axis=1, keepdims=True)
    return inverse * (grad_unit - along * unit_value)


def shards(features, proj_weight, text_embed, log_scale, logit_bias):
    zh, x, y, zq, zp, c = (lax.axis_index(name) for name in AXES)
    nx, ny, nq = (lax.axis_size(name) for name in ("x", "y", "zq"))
    emb = proj_weight.shape[1]
    block_rows = features.shape[0]
    own_rows = block_rows // nx
    text_rows = text_embed.shape[0]
    column_rows = nq * text_rows
    temper = jnp.exp(log_scale[0])
    logit_shift = logit_bias[0]

    partial_value = jnp.dot(features, proj_weight, preferred_element_type=F32).astype(BF)
    parts = exchange(partial_value.reshape(nx, own_rows, emb), "x")
    half_embed = jnp.sum(parts.astype(F32), axis=0)

    text_value = text_embed.astype(F32)
    text_inverse = lax.rsqrt(jnp.sum(text_value * text_value, axis=1, keepdims=True) + 1e-06)
    text_full = text_value * text_inverse
    text_unit = text_full.astype(BF)

    half_sent, text_unit = lax.optimization_barrier((half_embed.astype(BF), text_unit))
    other_half = flip(half_sent, "zh")
    text_far = gather(text_unit, ("zh", "zq")).reshape(2, column_rows, emb)
    text_both = jnp.stack(
        [lax.dynamic_index_in_dim(text_far, i, axis=0, keepdims=False) for i in (zh, 1 - zh)]
    )[:, None]
    text_both = jnp.concatenate([text_both, flip(text_both, "zp")], axis=1)[:, None]
    text_both = jnp.concatenate([text_both, flip(text_both, "c")], axis=1)
    text_block = text_both.reshape(8 * column_rows, emb)

    raw_embed = half_embed + other_half.astype(F32)
    image_inverse = lax.rsqrt(jnp.sum(raw_embed * raw_embed, axis=1, keepdims=True) + 1e-06)
    unit_full = raw_embed * image_inverse
    image_unit = unit_full.astype(BF)
    image_block = gather(image_unit, ("y", "x")).reshape(ny * block_rows, emb)

    def ids(first, second, third, fourth):
        return (((first * nq + second) * 2 + third) * 2) + fourth

    image_y = jnp.arange(ny, dtype=jnp.int32)[:, None]
    image_r = jnp.arange(block_rows, dtype=jnp.int32)[None, :]
    image_ids = (ids(image_y, zq, zp, c) * block_rows + image_r).reshape(-1, 1)

    def near_far(place, axis):
        shape = [1] * 5
        shape[axis] = 2
        return jnp.stack([place, 1 - place]).astype(jnp.int32).reshape(shape)

    text_q = jnp.arange(nq, dtype=jnp.int32).reshape(1, 1, 1, -1, 1)
    text_r = jnp.arange(text_rows, dtype=jnp.int32).reshape(1, 1, 1, 1, -1)
    text_group = (near_far(zh, 0) * nx + x) * ny + y
    text_ids = ids(text_group, text_q, near_far(zp, 2), near_far(c, 1)) * text_rows + text_r
    text_ids = text_ids.reshape(1, -1)

    logits = (
        temper
        * lax.dot_general(
            image_block, text_block, (((1,), (1,)), ((), ())), preferred_element_type=F32
        )
        + logit_shift
    )
    labels = jnp.where(image_ids == text_ids, 1.0, -1.0).astype(F32)
    coeffs = (-labels * jax.nn.sigmoid(-labels * logits) * temper).astype(BF)

    unit_part = jnp.dot(coeffs, text_block, preferred_element_type=F32).astype(BF)
    unit_parts = exchange(unit_part.reshape(ny * nx, own_rows, emb), ("y", "x"))

    text_part = lax.dot_general(
        coeffs[:, : 4 * column_rows],
        image_block,
        (((0,), (0,)), ((), ())),
        preferred_element_type=F32,
    )
    text_home = fold(fold(text_part, "c"), "zp").astype(BF).reshape(nq, text_rows, emb)
    unit_parts, text_home = lax.optimization_barrier((unit_parts, text_home))
    unit_grad = jnp.sum(unit_parts.astype(F32), axis=0)
    embed_rows = unit_backward(unit_grad, unit_full, image_inverse).astype(BF)
    embed_grad = gather(embed_rows, "x").reshape(block_rows, emb)

    width = emb // 2
    weight_part = jnp.stack(
        [
            lax.dot_general(
                features, half, (((0,), (0,)), ((), ())), preferred_element_type=F32
            ).astype(BF)
            for half in (embed_grad[:, :width], embed_grad[:, width:])
        ]
    )
    image_grad = lax.dot_general(
        embed_grad, proj_weight, (((1,), (1,)), ((), ())), preferred_element_type=F32
    ).astype(BF)

    near = ("zp", "y", "c")
    weight_rows = features.shape[1] // (ny * 2)
    weight_parts = exchange(weight_part.reshape(ny * 4, weight_rows, width), near)
    weight_sum = jnp.sum(weight_parts.astype(F32), axis=0).astype(BF)
    line_sent = jnp.concatenate(
        [
            jnp.broadcast_to(weight_sum[None], (nq, weight_rows, width)),
            text_home[:, :, :width],
            text_home[:, :, width:],
        ],
        axis=1,
    )
    line_sum = jnp.sum(exchange(line_sent, "zq").astype(F32), axis=0)
    weight_own = line_sum[:weight_rows].astype(BF)
    weight_grad = gather(weight_own, near).reshape(2, features.shape[1], width)
    weight_grad = jnp.concatenate([weight_grad[0], weight_grad[1]], axis=1)

    text_sum = line_sum[weight_rows:]
    text_unit_grad = jnp.concatenate([text_sum[:text_rows], text_sum[text_rows:]], axis=1)
    text_grad = unit_backward(text_unit_grad, text_full, text_inverse).astype(BF)
    return (image_grad, weight_grad, text_grad)


def solution(mesh):
    fine = Mesh(mesh.devices.reshape(SIZES), AXES)
    tp, dp = ("zh", "x"), ("y", "zq", "zp", "c")
    return jax.shard_map(
        shards,
        mesh=fine,
        in_specs=(P(dp, tp), P(tp, None), P(tp + dp, None), P(), P()),
        out_specs=(P(dp, tp), P(tp, None), P(tp + dp, None)),
        check_vma=False,
    )
```

time: 198 us -> 161 us (0.81)
  starting transfers between devices: 96.7 us -> 70 us
  waiting for transfers between devices: 56.7 us -> 44.9 us
  other arithmetic: 3.07 us -> 5.42 us
    all_to_all x7 -> x6, starting transfers between devices: 63 us -> 41.3 us  [exchange(): return lax.all_to_all(value, axes, 0, 0, tiled=False)]
    all_to_all x7 -> x6, waiting for transfers between devices: 45.1 us -> 26.3 us  [exchange(): return lax.all_to_all(value, axes, 0, 0, tiled=False)]
    ppermute x4 -> x5, waiting for transfers between devices: 11.7 us -> 18.6 us  [flip(): return lax.ppermute(value, axis, [(0, 1), (1, 0)])]
    ppermute x4 -> x5, starting transfers between devices: 33.6 us -> 28.7 us  [flip(): return lax.ppermute(value, axis, [(0, 1), (1, 0)])]
  transfers between devices with their start and end apart: 11 -> 11, of which waited for: 9 -> 8; matrix products, arithmetic and copies ran while one was open for 2% -> 4% of each run, Pallas kernels for 0% -> 0%
where the time goes in v3:
time: 161 us; the launch traced here: 160 us
  starting transfers between devices  70 us (43%)
  waiting for transfers between devices  44.9 us (28%)
  blocking collectives  27.7 us (17%)
  matrix products  6.22 us (4%)
  other arithmetic  5.42 us (3%)
  local copies, waits for them, and re-layouts  3.85 us (2%)
  between operations  2.24 us (1%)
    all_to_all x6, starting transfers between devices, exchange(): return lax.all_to_all(value, axes, 0, 0, tiled=False)  41.3 us
    ppermute x5, starting transfers between devices, flip(): return lax.ppermute(value, axis, [(0, 1), (1, 0)])  28.7 us
    all_to_all x2, blocking collectives, exchange(): return lax.all_to_all(value, axes, 0, 0, tiled=False)  27.7 us
    all_to_all x6, waiting for transfers between devices, exchange(): return lax.all_to_all(value, axes, 0, 0, tiled=False)  26.3 us
    ppermute x5, waiting for transfers between devices, flip(): return lax.ppermute(value, axis, [(0, 1), (1, 0)])  18.6 us
  transfers between devices with their start and end apart: 11, of which 8 were waited for; matrix products, arithmetic and copies ran while one was open for 4% of the time, Pallas kernels for 0%

profile of v3, /device:TPU:1, one launch (start us, length us, event | category | flops | bytes accessed | tf_op | source)
XLA Modules:
  0.0 160.3 jit_solution(8350229355487952540)
XLA Ops:
  1.6 1.8 %convolution_convert_fusion.1 = bf16[128,1024]{1,0:T(8,128)(2,1)} fusion(bf16[128,192]{0,1:T(8,128)(2,1)} %param.5, bf16[192,1024]{1,0:T(8,128)(2,1)S(1)} %copy-done), kind=kOutput, calls=%fused_computation.12 | convolution fusion | flops 50462720 | bytes 704512 | tf_op jit(solution)/shard_map/dot_general | solution.py:46
  3.4 4.8 %all-to-all-start = ((bf16[4,32,1024]{2,1,0:T(8,128)(2,1)}), bf16[4,32,1024]{2,1,0:T(8,128)(2,1)S(1)}, u32[]{:S(2)}, u32[]{:S(2)}) async-start(bf16[4,32,1024]{2,1,0:T(8,128)(2,1)} %bitcast), calls=%async_computation | async-start | bytes 524288 | tf_op jit(solution)/shard_map/all_to_all | solution.py:13
  8.5 5.2 %all-to-all-done = bf16[4,32,1024]{2,1,0:T(8,128)(2,1)S(1)} async-done(((bf16[4,32,1024]{2,1,0:T(8,128)(2,1)}), bf16[4,32,1024]{2,1,0:T(8,128)(2,1)S(1)}, u32[]{:S(2)}, u32[]{:S(2)}) %all-to-all-start) | async-done | bytes 262176 | tf_op jit(solution)/shard_map/all_to_all | solution.py:13
  14.5 14.8 %all-to-all-start.2 = ((bf16[8,16,1024]{2,1,0:T(8,128)(2,1)}), bf16[8,16,1024]{2,1,0:T(8,128)(2,1)S(1)}, u32[]{:S(2)}, u32[]{:S(2)}) async-start(bf16[8,16,1024]{2,1,0:T(8,128)(2,1)} %broadcast_in_dim.25), calls=%async_computation.2 | async-start | bytes 524288 | tf_op jit(solution)/shard_map/all_to_all | solution.py:13
  31.0 12.1 %collective-permute-start = (bf16[32,1024]{1,0:T(8,128)(2,1)S(1)}, bf16[32,1024]{1,0:T(8,128)(2,1)S(1)}, u32[]{:S(2)}, u32[]{:S(2)}) collective-permute-start(bf16[32,1024]{1,0:T(8,128)(2,1)S(1)} %convert_element_type.70), channel_id=1, source_target_pairs={{0,256},{256,0},{1,257},{257,1},{2,258},{258,2},{3,259},{259,3},{4... | collective-permute-start | bytes 196616 | tf_op jit(solution)/shard_map/ppermute | solution.py:22
  43.1 12.8 %collective-permute-done = bf16[32,1024]{1,0:T(8,128)(2,1)S(1)} collective-permute-done((bf16[32,1024]{1,0:T(8,128)(2,1)S(1)}, bf16[32,1024]{1,0:T(8,128)(2,1)S(1)}, u32[]{:S(2)}, u32[]{:S(2)}) %collective-permute-start) | collective-permute-done | bytes 65568 | tf_op jit(solution)/shard_map/ppermute | solution.py:22
  56.1 1.9 %collective-permute-start.1 = (bf16[2,1,64,1024]{3,2,1,0:T(8,128)(2,1)S(1)}, bf16[2,1,64,1024]{3,2,1,0:T(8,128)(2,1)S(1)}, u32[]{:S(2)}, u32[]{:S(2)}) collective-permute-start(bf16[2,1,64,1024]{3,2,1,0:T(8,128)(2,1)S(1)} %maximum_bitcast_fusion.1), channel_id=1, source_target_pairs={{0,2},{2,0},{1,3},{3,1},{4,6},{6,4},{5,7},{7,5},{8,10},{10,8},{9,1... | collective-permute-start | bytes 786440 | tf_op jit(solution)/shard_map/ppermute | solution.py:22
  59.2 4.9 %all-to-all-start.1 = ((bf16[16,32,1024]{2,1,0:T(8,128)(2,1)}), bf16[16,32,1024]{2,1,0:T(8,128)(2,1)S(1)}, u32[]{:S(2)}, u32[]{:S(2)}) async-start(bf16[16,32,1024]{2,1,0:T(8,128)(2,1)} %broadcast_in_dim.24), calls=%async_computation.1 | async-start | bytes 2097152 | tf_op jit(solution)/shard_map/all_to_all | solution.py:13
  64.2 5.1 %collective-permute-start.2 = (bf16[2,1,2,64,1024]{4,3,2,1,0:T(8,128)(2,1)S(1)}, bf16[2,1,2,64,1024]{4,3,2,1,0:T(8,128)(2,1)}, u32[]{:S(2)}, u32[]{:S(2)}) collective-permute-start(bf16[2,1,2,64,1024]{4,3,2,1,0:T(8,128)(2,1)S(1)} %maximum_bitcast_fusion), channel_id=1, source_target_pairs={{0,1},{1,0},{2,3},{3,2},{4,5},{5,4},{6,7},{7,6},{8,9},{9,8},{10,11... | collective-permute-start | bytes 1572872 | tf_op jit(solution)/shard_map/ppermute | solution.py:22
  69.6 1.4 collective-permute-done.2
  71.0 1.1 pad_maximum_fusion
  72.2 6.0 %all-to-all-done.1 = bf16[16,32,1024]{2,1,0:T(8,128)(2,1)S(1)} async-done(((bf16[16,32,1024]{2,1,0:T(8,128)(2,1)}), bf16[16,32,1024]{2,1,0:T(8,128)(2,1)S(1)}, u32[]{:S(2)}, u32[]{:S(2)}) %all-to-all-start.1) | async-done | bytes 1048608 | tf_op jit(solution)/shard_map/all_to_all | solution.py:13
  79.2 1.7 %convolution_convert_fusion = bf16[512,1024]{1,0:T(8,128)(2,1)} fusion(bf16[512,512]{1,0:T(8,128)(2,1)S(1)} %fusion.8, bf16[512,1024]{1,0:T(8,128)(2,1)S(1)} %bitcast.51), kind=kOutput, calls=%fused_computation.1 | convolution fusion | flops 537395200 | bytes 2621440 | tf_op jit(solution)/shard_map/dot_general | solution.py:99
  80.9 4.0 %all-to-all-start.3 = ((bf16[16,32,1024]{2,1,0:T(8,128)(2,1)}), bf16[16,32,1024]{2,1,0:T(8,128)(2,1)S(1)}, u32[]{:S(2)}, u32[]{:S(2)}) async-start(bf16[16,32,1024]{2,1,0:T(8,128)(2,1)} %bitcast.49), calls=%async_computation.3 | async-start | bytes 2097152 | tf_op jit(solution)/shard_map/all_to_all | solution.py:13
  85.4 6.2 %collective-permute-start.3 = (bf16[128,1024]{1,0:T(8,128)(2,1)S(1)}, bf16[128,1024]{1,0:T(8,128)(2,1)S(1)}, u32[]{:S(2)}, u32[]{:S(2)}) collective-permute-start(bf16[128,1024]{1,0:T(8,128)(2,1)S(1)} %slice.89), channel_id=1, source_target_pairs={{0,1},{1,0},{2,3},{3,2},{4,5},{5,4},{6,7},{7,6},{8,9},{9,8},{10,11... | collective-permute-start | bytes 786440 | tf_op jit(solution)/shard_map/ppermute | solution.py:22
  91.6 1.1 collective-permute-done.3
  92.8 3.3 %collective-permute-start.4 = (bf16[64,1024]{1,0:T(8,128)(2,1)S(1)}, bf16[64,1024]{1,0:T(8,128)(2,1)S(1)}, u32[]{:S(2)}, u32[]{:S(2)}) collective-permute-start(bf16[64,1024]{1,0:T(8,128)(2,1)S(1)} %slice.90), channel_id=1, source_target_pairs={{0,2},{2,0},{1,3},{3,1},{4,6},{6,4},{5,7},{7,5},{8,10},{10,8},{9,1... | collective-permute-start | bytes 393224 | tf_op jit(solution)/shard_map/ppermute | solution.py:22
  96.2 3.3 %collective-permute-done.4 = bf16[64,1024]{1,0:T(8,128)(2,1)S(1)} collective-permute-done((bf16[64,1024]{1,0:T(8,128)(2,1)S(1)}, bf16[64,1024]{1,0:T(8,128)(2,1)S(1)}, u32[]{:S(2)}, u32[]{:S(2)}) %collective-permute-start.4) | collective-permute-done | bytes 131104 | tf_op jit(solution)/shard_map/ppermute | solution.py:22
  100.0 9.6 %all_to_all.40 = bf16[4,32,1024]{2,1,0:T(8,128)(2,1)S(1)} all-to-all(bf16[4,32,1024]{2,1,0:T(8,128)(2,1)S(1)} %broadcast_in_dim.28), channel_id=1, replica_groups=mesh['zh'=2,'x'=4,'y'=4,'zq'=4,'zp'=2,'c'=2] {'x'}, dimensions={0} | all-to-all | bytes 524288 | tf_op jit(solution)/shard_map/all_to_all | solution.py:13
  110.8 8.1 %all-to-all-start.5 = ((bf16[16,24,512]{2,1,0:T(8,128)(2,1)}), bf16[16,24,512]{2,1,0:T(8,128)(2,1)S(1)}, u32[]{:S(2)}, u32[]{:S(2)}) async-start(bf16[16,24,512]{2,1,0:T(8,128)(2,1)} %bitcast.22), calls=%async_computation.5 | async-start | bytes 786432 | tf_op jit(solution)/shard_map/all_to_all | solution.py:13
  118.9 8.4 %all-to-all-done.5 = bf16[16,24,512]{2,1,0:T(8,128)(2,1)S(1)} async-done(((bf16[16,24,512]{2,1,0:T(8,128)(2,1)}), bf16[16,24,512]{2,1,0:T(8,128)(2,1)S(1)}, u32[]{:S(2)}, u32[]{:S(2)}) %all-to-all-start.5) | async-done | bytes 393248 | tf_op jit(solution)/shard_map/all_to_all | solution.py:13
  127.4 18.0 %all_to_all.41 = bf16[4,56,512]{2,1,0:T(8,128)(2,1)S(1)} all-to-all(bf16[4,56,512]{2,1,0:T(8,128)(2,1)S(1)} %pad_maximum_fusion.3), channel_id=1, replica_groups=mesh['zh'=2,'x'=4,'y'=4,'zq'=4,'zp'=2,'c'=2] {'zq'}, dimensions={0} | all-to-all | bytes 458752 | tf_op jit(solution)/shard_map/all_to_all | solution.py:13
  146.3 4.7 %all-to-all-start.7 = ((bf16[16,24,512]{2,1,0:T(8,128)(2,1)}), bf16[16,24,512]{2,1,0:T(8,128)(2,1)S(1)}, u32[]{:S(2)}, u32[]{:S(2)}) async-start(bf16[16,24,512]{2,1,0:T(8,128)(2,1)} %broadcast_in_dim.30), calls=%async_computation.7 | async-start | bytes 786432 | tf_op jit(solution)/shard_map/all_to_all | solution.py:13
  152.8 6.7 %all-to-all-done.7 = bf16[16,24,512]{2,1,0:T(8,128)(2,1)S(1)} async-done(((bf16[16,24,512]{2,1,0:T(8,128)(2,1)}), bf16[16,24,512]{2,1,0:T(8,128)(2,1)S(1)}, u32[]{:S(2)}, u32[]{:S(2)}) %all-to-all-start.7) | async-done | bytes 393248 | tf_op jit(solution)/shard_map/all_to_all | solution.py:13
  (62 shorter events, 10.9 us)
Async XLA Ops:
  0.6 1.0 copy-start
  0.6 7.6 %copy-start.1 = (bf16[16,1024]{1,0:T(8,128)(2,1)S(1)}, bf16[16,1024]{1,0:T(8,128)(2,1)}, u32[]{:S(2)}) copy-start(bf16[16,1024]{1,0:T(8,128)(2,1)} %param.7) | copy-start | bytes 98308
  3.4 10.4 %all-to-all-start = ((bf16[4,32,1024]{2,1,0:T(8,128)(2,1)}), bf16[4,32,1024]{2,1,0:T(8,128)(2,1)S(1)}, u32[]{:S(2)}, u32[]{:S(2)}) async-start(bf16[4,32,1024]{2,1,0:T(8,128)(2,1)} %bitcast), calls=%async_computation | async-start | bytes 524288 | tf_op jit(solution)/shard_map/all_to_all | solution.py:13
  14.5 41.5 %all-to-all-start.2 = ((bf16[8,16,1024]{2,1,0:T(8,128)(2,1)}), bf16[8,16,1024]{2,1,0:T(8,128)(2,1)S(1)}, u32[]{:S(2)}, u32[]{:S(2)}) async-start(bf16[8,16,1024]{2,1,0:T(8,128)(2,1)} %broadcast_in_dim.25), calls=%async_computation.2 | async-start | bytes 524288 | tf_op jit(solution)/shard_map/all_to_all | solution.py:13
  31.0 24.9 %collective-permute-start = (bf16[32,1024]{1,0:T(8,128)(2,1)S(1)}, bf16[32,1024]{1,0:T(8,128)(2,1)S(1)}, u32[]{:S(2)}, u32[]{:S(2)}) collective-permute-start(bf16[32,1024]{1,0:T(8,128)(2,1)S(1)} %convert_element_type.70), channel_id=1, source_target_pairs={{0,256},{256,0},{1,257},{257,1},{2,258},{258,2},{3,259},{259,3},{4... | collective-permute-start | bytes 196616 | tf_op jit(solution)/shard_map/ppermute | solution.py:22
  56.1 8.1 %collective-permute-start.1 = (bf16[2,1,64,1024]{3,2,1,0:T(8,128)(2,1)S(1)}, bf16[2,1,64,1024]{3,2,1,0:T(8,128)(2,1)S(1)}, u32[]{:S(2)}, u32[]{:S(2)}) collective-permute-start(bf16[2,1,64,1024]{3,2,1,0:T(8,128)(2,1)S(1)} %maximum_bitcast_fusion.1), channel_id=1, source_target_pairs={{0,2},{2,0},{1,3},{3,1},{4,6},{6,4},{5,7},{7,5},{8,10},{10,8},{9,1... | collective-permute-start | bytes 786440 | tf_op jit(solution)/shard_map/ppermute | solution.py:22
  59.2 18.9 %all-to-all-start.1 = ((bf16[16,32,1024]{2,1,0:T(8,128)(2,1)}), bf16[16,32,1024]{2,1,0:T(8,128)(2,1)S(1)}, u32[]{:S(2)}, u32[]{:S(2)}) async-start(bf16[16,32,1024]{2,1,0:T(8,128)(2,1)} %broadcast_in_dim.24), calls=%async_computation.1 | async-start | bytes 2097152 | tf_op jit(solution)/shard_map/all_to_all | solution.py:13
  64.2 6.8 %collective-permute-start.2 = (bf16[2,1,2,64,1024]{4,3,2,1,0:T(8,128)(2,1)S(1)}, bf16[2,1,2,64,1024]{4,3,2,1,0:T(8,128)(2,1)}, u32[]{:S(2)}, u32[]{:S(2)}) collective-permute-start(bf16[2,1,2,64,1024]{4,3,2,1,0:T(8,128)(2,1)S(1)} %maximum_bitcast_fusion), channel_id=1, source_target_pairs={{0,1},{1,0},{2,3},{3,2},{4,5},{5,4},{6,7},{7,6},{8,9},{9,8},{10,11... | collective-permute-start | bytes 1572872 | tf_op jit(solution)/shard_map/ppermute | solution.py:22
  79.2 1.7 %copy-start.3 = (bf16[512,512]{1,0:T(8,128)(2,1)}, bf16[512,512]{1,0:T(8,128)(2,1)S(1)}, u32[]{:S(2)}) copy-start(bf16[512,512]{1,0:T(8,128)(2,1)S(1)} %fusion.8) | copy-start | bytes 1572868
  80.9 4.0 %copy-start.4 = (bf16[512,512]{1,0:T(8,128)(2,1)S(1)}, bf16[512,512]{1,0:T(8,128)(2,1)}, u32[]{:S(2)}) copy-start(bf16[512,512]{1,0:T(8,128)(2,1)} %copy-done.3) | copy-start | bytes 1572868
  80.9 18.6 %all-to-all-start.3 = ((bf16[16,32,1024]{2,1,0:T(8,128)(2,1)}), bf16[16,32,1024]{2,1,0:T(8,128)(2,1)S(1)}, u32[]{:S(2)}, u32[]{:S(2)}) async-start(bf16[16,32,1024]{2,1,0:T(8,128)(2,1)} %bitcast.49), calls=%async_computation.3 | async-start | bytes 2097152 | tf_op jit(solution)/shard_map/all_to_all | solution.py:13
  85.4 7.4 %collective-permute-start.3 = (bf16[128,1024]{1,0:T(8,128)(2,1)S(1)}, bf16[128,1024]{1,0:T(8,128)(2,1)S(1)}, u32[]{:S(2)}, u32[]{:S(2)}) collective-permute-start(bf16[128,1024]{1,0:T(8,128)(2,1)S(1)} %slice.89), channel_id=1, source_target_pairs={{0,1},{1,0},{2,3},{3,2},{4,5},{5,4},{6,7},{7,6},{8,9},{9,8},{10,11... | collective-permute-start | bytes 786440 | tf_op jit(solution)/shard_map/ppermute | solution.py:22
  92.8 6.6 %collective-permute-start.4 = (bf16[64,1024]{1,0:T(8,128)(2,1)S(1)}, bf16[64,1024]{1,0:T(8,128)(2,1)S(1)}, u32[]{:S(2)}, u32[]{:S(2)}) collective-permute-start(bf16[64,1024]{1,0:T(8,128)(2,1)S(1)} %slice.90), channel_id=1, source_target_pairs={{0,2},{2,0},{1,3},{3,1},{4,6},{6,4},{5,7},{7,5},{8,10},{10,8},{9,1... | collective-permute-start | bytes 393224 | tf_op jit(solution)/shard_map/ppermute | solution.py:22
  99.7 10.0 %copy-start.2 = (bf16[128,192]{0,1:T(8,128)(2,1)S(1)}, bf16[128,192]{0,1:T(8,128)(2,1)}, u32[]{:S(2)}) copy-start(bf16[128,192]{0,1:T(8,128)(2,1)} %param.5) | copy-start | bytes 147460
  110.8 16.5 %all-to-all-start.5 = ((bf16[16,24,512]{2,1,0:T(8,128)(2,1)}), bf16[16,24,512]{2,1,0:T(8,128)(2,1)S(1)}, u32[]{:S(2)}, u32[]{:S(2)}) async-start(bf16[16,24,512]{2,1,0:T(8,128)(2,1)} %bitcast.22), calls=%async_computation.5 | async-start | bytes 786432 | tf_op jit(solution)/shard_map/all_to_all | solution.py:13
  146.3 13.2 %all-to-all-start.7 = ((bf16[16,24,512]{2,1,0:T(8,128)(2,1)}), bf16[16,24,512]{2,1,0:T(8,128)(2,1)S(1)}, u32[]{:S(2)}, u32[]{:S(2)}) async-start(bf16[16,24,512]{2,1,0:T(8,128)(2,1)} %broadcast_in_dim.30), calls=%async_computation.7 | async-start | bytes 786432 | tf_op jit(solution)/shard_map/all_to_all | solution.py:13

commit v4 on v3

--- a/solution.py
+++ b/solution.py
@@ -44,16 +44,19 @@
     logit_shift = logit_bias[0]
 
     partial_value = jnp.dot(features, proj_weight, preferred_element_type=F32).astype(BF)
-    parts = exchange(partial_value.reshape(nx, own_rows, emb), "x")
-    half_embed = jnp.sum(parts.astype(F32), axis=0)
+    parts = partial_value.reshape(nx, own_rows, emb)
+    half_embed = lax.dynamic_index_in_dim(parts, x, axis=0, keepdims=False).astype(F32)
+    for step in (2, 1, 3):
+        ring = [(i, (i + step) % nx) for i in range(nx)]
+        away = lax.dynamic_index_in_dim(parts, (x + step) % nx, axis=0, keepdims=False)
+        half_embed = half_embed + lax.ppermute(away, "x", ring).astype(F32)
 
     text_value = text_embed.astype(F32)
     text_inverse = lax.rsqrt(jnp.sum(text_value * text_value, axis=1, keepdims=True) + 1e-06)
     text_full = text_value * text_inverse
     text_unit = text_full.astype(BF)
 
-    half_sent, text_unit = lax.optimization_barrier((half_embed.astype(BF), text_unit))
-    other_half = flip(half_sent, "zh")
+    other_half = flip(half_embed.astype(BF), "zh")
     text_far = gather(text_unit, ("zh", "zq")).reshape(2, column_rows, emb)
     text_both = jnp.stack(
         [lax.dynamic_index_in_dim(text_far, i, axis=0, keepdims=False) for i in (zh, 1 - zh)]

time: 161 us -> 160 us (level)
  waiting for transfers between devices: 44.9 us -> 28 us
  starting transfers between devices: 70 us -> 79.1 us
  blocking collectives: 27.7 us -> 34.7 us
    ppermute x5, waiting for transfers between devices: 18.6 us -> 7.27 us  [flip(): return lax.ppermute(value, axis, [(0, 1), (1, 0)])]
    ppermute x0 -> x3, starting transfers between devices: none -> 9.93 us  [shards(): half_embed = half_embed + lax.ppermute(away, 'x', ring).astype(F32)]
    all_to_all x6 -> x5, waiting for transfers between devices: 26.3 us -> 17 us  [exchange(): return lax.all_to_all(value, axes, 0, 0, tiled=False)]
    all_to_all x2, blocking collectives: 27.7 us -> 34.7 us  [exchange(): return lax.all_to_all(value, axes, 0, 0, tiled=False)]
    ppermute x0 -> x3, waiting for transfers between devices: none -> 3.75 us  [shards(): half_embed = half_embed + lax.ppermute(away, 'x', ring).astype(F32)]
    all_to_all x6 -> x5, starting transfers between devices: 41.3 us -> 37.8 us  [exchange(): return lax.all_to_all(value, axes, 0, 0, tiled=False)]
    ppermute x5, starting transfers between devices: 28.7 us -> 31.3 us  [flip(): return lax.ppermute(value, axis, [(0, 1), (1, 0)])]
  transfers between devices with their start and end apart: 11 -> 13, of which waited for: 8 -> 8; matrix products, arithmetic and copies ran while one was open for 4% -> 4% of each run, Pallas kernels for 0% -> 0%
where the time goes in v4:
time: 160 us; the launch traced here: 159 us
  starting transfers between devices  79.1 us (49%)
  blocking collectives  34.7 us (22%)
  waiting for transfers between devices  28 us (18%)
  other arithmetic  6.93 us (4%)
  matrix products  4.7 us (3%)
  local copies, waits for them, and re-layouts  2.89 us (2%)
  between operations  2.29 us (1%)
    all_to_all x5, starting transfers between devices, exchange(): return lax.all_to_all(value, axes, 0, 0, tiled=False)  37.8 us
    all_to_all x2, blocking collectives, exchange(): return lax.all_to_all(value, axes, 0, 0, tiled=False)  34.7 us
    ppermute x5, starting transfers between devices, flip(): return lax.ppermute(value, axis, [(0, 1), (1, 0)])  31.3 us
    all_to_all x5, waiting for transfers between devices, exchange(): return lax.all_to_all(value, axes, 0, 0, tiled=False)  17 us
    ppermute x3, starting transfers between devices, shards(): half_embed = half_embed + lax.ppermute(away, 'x', ring).astype(F32)  9.93 us
    ppermute x5, waiting for transfers between devices, flip(): return lax.ppermute(value, axis, [(0, 1), (1, 0)])  7.27 us
    ppermute x3, waiting for transfers between devices, shards(): half_embed = half_embed + lax.ppermute(away, 'x', ring).astype(F32)  3.75 us
  transfers between devices with their start and end apart: 13, of which 8 were waited for; matrix products, arithmetic and copies ran while one was open for 4% of the time, Pallas kernels for 0%

profile of v4, /device:TPU:1, one launch (start us, length us, event | category | flops | bytes accessed | tf_op | source)
XLA Modules:
  0.0 158.6 jit_solution(17983868106726033385)
XLA Ops:
  3.2 15.6 %all-to-all-start.1 = ((bf16[8,16,1024]{2,1,0:T(8,128)(2,1)}), bf16[8,16,1024]{2,1,0:T(8,128)(2,1)S(1)}, u32[]{:S(2)}, u32[]{:S(2)}) async-start(bf16[8,16,1024]{2,1,0:T(8,128)(2,1)} %broadcast_in_dim.25), calls=%async_computation.1 | async-start | bytes 524288 | tf_op jit(solution)/shard_map/all_to_all | solution.py:13
  19.1 4.7 %collective-permute-start = (bf16[32,1024]{1,0:T(8,128)(2,1)S(1)}, bf16[32,1024]{1,0:T(8,128)(2,1)S(1)}, u32[]{:S(2)}, u32[]{:S(2)}) collective-permute-start(bf16[32,1024]{1,0:T(8,128)(2,1)S(1)} %get-tuple-element.13), channel_id=1, source_target_pairs={{0,128},{64,192},{128,0},{192,64},{1,129},{65,193},{129,1},{193,65... | collective-permute-start | bytes 196616 | tf_op jit(solution)/shard_map/ppermute | solution.py:52
  23.8 2.8 %collective-permute-start.2 = (bf16[32,1024]{1,0:T(8,128)(2,1)S(1)}, bf16[32,1024]{1,0:T(8,128)(2,1)S(1)}, u32[]{:S(2)}, u32[]{:S(2)}) collective-permute-start(bf16[32,1024]{1,0:T(8,128)(2,1)S(1)} %get-tuple-element.14), channel_id=1, source_target_pairs={{0,192},{64,0},{128,64},{192,128},{1,193},{65,1},{129,65},{193,129... | collective-permute-start | bytes 196616 | tf_op jit(solution)/shard_map/ppermute | solution.py:52
  26.5 2.5 %collective-permute-start.1 = (bf16[32,1024]{1,0:T(8,128)(2,1)S(1)}, bf16[32,1024]{1,0:T(8,128)(2,1)S(1)}, u32[]{:S(2)}, u32[]{:S(2)}) collective-permute-start(bf16[32,1024]{1,0:T(8,128)(2,1)S(1)} %get-tuple-element.15), channel_id=1, source_target_pairs={{0,64},{64,128},{128,192},{192,0},{1,65},{65,129},{129,193},{193,1... | collective-permute-start | bytes 196616 | tf_op jit(solution)/shard_map/ppermute | solution.py:52
  29.3 3.7 %collective-permute-done.1 = bf16[32,1024]{1,0:T(8,128)(2,1)S(1)} collective-permute-done((bf16[32,1024]{1,0:T(8,128)(2,1)S(1)}, bf16[32,1024]{1,0:T(8,128)(2,1)S(1)}, u32[]{:S(2)}, u32[]{:S(2)}) %collective-permute-start.1) | collective-permute-done | bytes 65568 | tf_op jit(solution)/shard_map/ppermute | solution.py:52
  33.1 11.8 %collective-permute-start.3 = (bf16[32,1024]{1,0:T(8,128)(2,1)S(1)}, bf16[32,1024]{1,0:T(8,128)(2,1)S(1)}, u32[]{:S(2)}, u32[]{:S(2)}) collective-permute-start(bf16[32,1024]{1,0:T(8,128)(2,1)S(1)} %fusion.26), channel_id=1, source_target_pairs={{0,256},{256,0},{1,257},{257,1},{2,258},{258,2},{3,259},{259,3},{4... | collective-permute-start | bytes 196616 | tf_op jit(solution)/shard_map/ppermute | solution.py:22
  47.3 2.6 %collective-permute-start.4 = (bf16[2,1,64,1024]{3,2,1,0:T(8,128)(2,1)S(1)}, bf16[2,1,64,1024]{3,2,1,0:T(8,128)(2,1)S(1)}, u32[]{:S(2)}, u32[]{:S(2)}) collective-permute-start(bf16[2,1,64,1024]{3,2,1,0:T(8,128)(2,1)S(1)} %maximum_bitcast_fusion.1), channel_id=1, source_target_pairs={{0,2},{2,0},{1,3},{3,1},{4,6},{6,4},{5,7},{7,5},{8,10},{10,8},{9,1... | collective-permute-start | bytes 786440 | tf_op jit(solution)/shard_map/ppermute | solution.py:22
  51.0 4.9 %all-to-all-start = ((bf16[16,32,1024]{2,1,0:T(8,128)(2,1)}), bf16[16,32,1024]{2,1,0:T(8,128)(2,1)S(1)}, u32[]{:S(2)}, u32[]{:S(2)}) async-start(bf16[16,32,1024]{2,1,0:T(8,128)(2,1)} %broadcast_in_dim.24), calls=%async_computation | async-start | bytes 2097152 | tf_op jit(solution)/shard_map/all_to_all | solution.py:13
  56.1 7.4 %collective-permute-start.5 = (bf16[2,1,2,64,1024]{4,3,2,1,0:T(8,128)(2,1)S(1)}, bf16[2,1,2,64,1024]{4,3,2,1,0:T(8,128)(2,1)}, u32[]{:S(2)}, u32[]{:S(2)}) collective-permute-start(bf16[2,1,2,64,1024]{4,3,2,1,0:T(8,128)(2,1)S(1)} %maximum_bitcast_fusion), channel_id=1, source_target_pairs={{0,1},{1,0},{2,3},{3,2},{4,5},{5,4},{6,7},{7,6},{8,9},{9,8},{10,11... | collective-permute-start | bytes 1572872 | tf_op jit(solution)/shard_map/ppermute | solution.py:22
  63.7 1.4 collective-permute-done.5
  65.1 1.1 pad_maximum_fusion
  66.3 1.9 %all-to-all-done = bf16[16,32,1024]{2,1,0:T(8,128)(2,1)S(1)} async-done(((bf16[16,32,1024]{2,1,0:T(8,128)(2,1)}), bf16[16,32,1024]{2,1,0:T(8,128)(2,1)S(1)}, u32[]{:S(2)}, u32[]{:S(2)}) %all-to-all-start) | async-done | bytes 1048608 | tf_op jit(solution)/shard_map/all_to_all | solution.py:13
  69.3 1.7 %convolution_convert_fusion = bf16[512,1024]{1,0:T(8,128)(2,1)} fusion(bf16[512,512]{1,0:T(8,128)(2,1)S(1)} %fusion.8, bf16[512,1024]{1,0:T(8,128)(2,1)S(1)} %bitcast.68), kind=kOutput, calls=%fused_computation.1 | convolution fusion | flops 537395200 | bytes 2621440 | tf_op jit(solution)/shard_map/dot_general | solution.py:102
  71.0 5.1 %all-to-all-start.2 = ((bf16[16,32,1024]{2,1,0:T(8,128)(2,1)}), bf16[16,32,1024]{2,1,0:T(8,128)(2,1)S(1)}, u32[]{:S(2)}, u32[]{:S(2)}) async-start(bf16[16,32,1024]{2,1,0:T(8,128)(2,1)} %bitcast.66), calls=%async_computation.2 | async-start | bytes 2097152 | tf_op jit(solution)/shard_map/all_to_all | solution.py:13
  76.6 6.9 %collective-permute-start.6 = (bf16[128,1024]{1,0:T(8,128)(2,1)S(1)}, bf16[128,1024]{1,0:T(8,128)(2,1)S(1)}, u32[]{:S(2)}, u32[]{:S(2)}) collective-permute-start(bf16[128,1024]{1,0:T(8,128)(2,1)S(1)} %slice.89), channel_id=1, source_target_pairs={{0,1},{1,0},{2,3},{3,2},{4,5},{5,4},{6,7},{7,6},{8,9},{9,8},{10,11... | collective-permute-start | bytes 786440 | tf_op jit(solution)/shard_map/ppermute | solution.py:22
  83.6 1.1 collective-permute-done.6
  84.8 2.6 %collective-permute-start.7 = (bf16[64,1024]{1,0:T(8,128)(2,1)S(1)}, bf16[64,1024]{1,0:T(8,128)(2,1)S(1)}, u32[]{:S(2)}, u32[]{:S(2)}) collective-permute-start(bf16[64,1024]{1,0:T(8,128)(2,1)S(1)} %slice.90), channel_id=1, source_target_pairs={{0,2},{2,0},{1,3},{3,1},{4,6},{6,4},{5,7},{7,5},{8,10},{10,8},{9,1... | collective-permute-start | bytes 393224 | tf_op jit(solution)/shard_map/ppermute | solution.py:22
  87.5 4.0 %collective-permute-done.7 = bf16[64,1024]{1,0:T(8,128)(2,1)S(1)} collective-permute-done((bf16[64,1024]{1,0:T(8,128)(2,1)S(1)}, bf16[64,1024]{1,0:T(8,128)(2,1)S(1)}, u32[]{:S(2)}, u32[]{:S(2)}) %collective-permute-start.7) | collective-permute-done | bytes 131104 | tf_op jit(solution)/shard_map/ppermute | solution.py:22
  92.0 9.6 %all_to_all.35 = bf16[4,32,1024]{2,1,0:T(8,128)(2,1)S(1)} all-to-all(bf16[4,32,1024]{2,1,0:T(8,128)(2,1)S(1)} %broadcast_in_dim.28), channel_id=1, replica_groups=mesh['zh'=2,'x'=4,'y'=4,'zq'=4,'zp'=2,'c'=2] {'x'}, dimensions={0} | all-to-all | bytes 524288 | tf_op jit(solution)/shard_map/all_to_all | solution.py:13
  102.8 7.4 %all-to-all-start.4 = ((bf16[16,24,512]{2,1,0:T(8,128)(2,1)}), bf16[16,24,512]{2,1,0:T(8,128)(2,1)S(1)}, u32[]{:S(2)}, u32[]{:S(2)}) async-start(bf16[16,24,512]{2,1,0:T(8,128)(2,1)} %bitcast.26), calls=%async_computation.4 | async-start | bytes 786432 | tf_op jit(solution)/shard_map/all_to_all | solution.py:13
  110.2 8.4 %all-to-all-done.4 = bf16[16,24,512]{2,1,0:T(8,128)(2,1)S(1)} async-done(((bf16[16,24,512]{2,1,0:T(8,128)(2,1)}), bf16[16,24,512]{2,1,0:T(8,128)(2,1)S(1)}, u32[]{:S(2)}, u32[]{:S(2)}) %all-to-all-start.4) | async-done | bytes 393248 | tf_op jit(solution)/shard_map/all_to_all | solution.py:13
  118.7 25.0 %all_to_all.36 = bf16[4,56,512]{2,1,0:T(8,128)(2,1)S(1)} all-to-all(bf16[4,56,512]{2,1,0:T(8,128)(2,1)S(1)} %pad_maximum_fusion.3), channel_id=1, replica_groups=mesh['zh'=2,'x'=4,'y'=4,'zq'=4,'zp'=2,'c'=2] {'zq'}, dimensions={0} | all-to-all | bytes 458752 | tf_op jit(solution)/shard_map/all_to_all | solution.py:13
  144.5 4.8 %all-to-all-start.6 = ((bf16[16,24,512]{2,1,0:T(8,128)(2,1)}), bf16[16,24,512]{2,1,0:T(8,128)(2,1)S(1)}, u32[]{:S(2)}, u32[]{:S(2)}) async-start(bf16[16,24,512]{2,1,0:T(8,128)(2,1)} %broadcast_in_dim.30), calls=%async_computation.6 | async-start | bytes 786432 | tf_op jit(solution)/shard_map/all_to_all | solution.py:13
  151.1 6.7 %all-to-all-done.6 = bf16[16,24,512]{2,1,0:T(8,128)(2,1)S(1)} async-done(((bf16[16,24,512]{2,1,0:T(8,128)(2,1)}), bf16[16,24,512]{2,1,0:T(8,128)(2,1)S(1)}, u32[]{:S(2)}, u32[]{:S(2)}) %all-to-all-start.6) | async-done | bytes 393248 | tf_op jit(solution)/shard_map/all_to_all | solution.py:13
  (65 shorter events, 12.5 us)
Async XLA Ops:
  0.6 18.2 %copy-start = (bf16[192,1024]{1,0:T(8,128)(2,1)S(1)}, bf16[192,1024]{1,0:T(8,128)(2,1)}, u32[]{:S(2)}) copy-start(bf16[192,1024]{1,0:T(8,128)(2,1)} %param.6) | copy-start | bytes 1179652
  0.6 18.2 %copy-start.2 = (bf16[128,192]{0,1:T(8,128)(2,1)S(1)}, bf16[128,192]{0,1:T(8,128)(2,1)}, u32[]{:S(2)}) copy-start(bf16[128,192]{0,1:T(8,128)(2,1)} %param.5) | copy-start | bytes 147460
  3.2 44.1 %all-to-all-start.1 = ((bf16[8,16,1024]{2,1,0:T(8,128)(2,1)}), bf16[8,16,1024]{2,1,0:T(8,128)(2,1)S(1)}, u32[]{:S(2)}, u32[]{:S(2)}) async-start(bf16[8,16,1024]{2,1,0:T(8,128)(2,1)} %broadcast_in_dim.25), calls=%async_computation.1 | async-start | bytes 524288 | tf_op jit(solution)/shard_map/all_to_all | solution.py:13
  19.1 10.2 %collective-permute-start = (bf16[32,1024]{1,0:T(8,128)(2,1)S(1)}, bf16[32,1024]{1,0:T(8,128)(2,1)S(1)}, u32[]{:S(2)}, u32[]{:S(2)}) collective-permute-start(bf16[32,1024]{1,0:T(8,128)(2,1)S(1)} %get-tuple-element.13), channel_id=1, source_target_pairs={{0,128},{64,192},{128,0},{192,64},{1,129},{65,193},{129,1},{193,65... | collective-permute-start | bytes 196616 | tf_op jit(solution)/shard_map/ppermute | solution.py:52
  23.8 5.5 %collective-permute-start.2 = (bf16[32,1024]{1,0:T(8,128)(2,1)S(1)}, bf16[32,1024]{1,0:T(8,128)(2,1)S(1)}, u32[]{:S(2)}, u32[]{:S(2)}) collective-permute-start(bf16[32,1024]{1,0:T(8,128)(2,1)S(1)} %get-tuple-element.14), channel_id=1, source_target_pairs={{0,192},{64,0},{128,64},{192,128},{1,193},{65,1},{129,65},{193,129... | collective-permute-start | bytes 196616 | tf_op jit(solution)/shard_map/ppermute | solution.py:52
  26.5 6.5 %collective-permute-start.1 = (bf16[32,1024]{1,0:T(8,128)(2,1)S(1)}, bf16[32,1024]{1,0:T(8,128)(2,1)S(1)}, u32[]{:S(2)}, u32[]{:S(2)}) collective-permute-start(bf16[32,1024]{1,0:T(8,128)(2,1)S(1)} %get-tuple-element.15), channel_id=1, source_target_pairs={{0,64},{64,128},{128,192},{192,0},{1,65},{65,129},{129,193},{193,1... | collective-permute-start | bytes 196616 | tf_op jit(solution)/shard_map/ppermute | solution.py:52
  33.1 14.0 %collective-permute-start.3 = (bf16[32,1024]{1,0:T(8,128)(2,1)S(1)}, bf16[32,1024]{1,0:T(8,128)(2,1)S(1)}, u32[]{:S(2)}, u32[]{:S(2)}) collective-permute-start(bf16[32,1024]{1,0:T(8,128)(2,1)S(1)} %fusion.26), channel_id=1, source_target_pairs={{0,256},{256,0},{1,257},{257,1},{2,258},{258,2},{3,259},{259,3},{4... | collective-permute-start | bytes 196616 | tf_op jit(solution)/shard_map/ppermute | solution.py:22
  47.3 8.7 %collective-permute-start.4 = (bf16[2,1,64,1024]{3,2,1,0:T(8,128)(2,1)S(1)}, bf16[2,1,64,1024]{3,2,1,0:T(8,128)(2,1)S(1)}, u32[]{:S(2)}, u32[]{:S(2)}) collective-permute-start(bf16[2,1,64,1024]{3,2,1,0:T(8,128)(2,1)S(1)} %maximum_bitcast_fusion.1), channel_id=1, source_target_pairs={{0,2},{2,0},{1,3},{3,1},{4,6},{6,4},{5,7},{7,5},{8,10},{10,8},{9,1... | collective-permute-start | bytes 786440 | tf_op jit(solution)/shard_map/ppermute | solution.py:22
  51.0 17.2 %all-to-all-start = ((bf16[16,32,1024]{2,1,0:T(8,128)(2,1)}), bf16[16,32,1024]{2,1,0:T(8,128)(2,1)S(1)}, u32[]{:S(2)}, u32[]{:S(2)}) async-start(bf16[16,32,1024]{2,1,0:T(8,128)(2,1)} %broadcast_in_dim.24), calls=%async_computation | async-start | bytes 2097152 | tf_op jit(solution)/shard_map/all_to_all | solution.py:13
  56.1 9.1 %collective-permute-start.5 = (bf16[2,1,2,64,1024]{4,3,2,1,0:T(8,128)(2,1)S(1)}, bf16[2,1,2,64,1024]{4,3,2,1,0:T(8,128)(2,1)}, u32[]{:S(2)}, u32[]{:S(2)}) collective-permute-start(bf16[2,1,2,64,1024]{4,3,2,1,0:T(8,128)(2,1)S(1)} %maximum_bitcast_fusion), channel_id=1, source_target_pairs={{0,1},{1,0},{2,3},{3,2},{4,5},{5,4},{6,7},{7,6},{8,9},{9,8},{10,11... | collective-permute-start | bytes 1572872 | tf_op jit(solution)/shard_map/ppermute | solution.py:22
  69.3 1.7 %copy-start.3 = (bf16[512,512]{1,0:T(8,128)(2,1)}, bf16[512,512]{1,0:T(8,128)(2,1)S(1)}, u32[]{:S(2)}) copy-start(bf16[512,512]{1,0:T(8,128)(2,1)S(1)} %fusion.8) | copy-start | bytes 1572868
  71.0 5.2 %copy-start.4 = (bf16[512,512]{1,0:T(8,128)(2,1)S(1)}, bf16[512,512]{1,0:T(8,128)(2,1)}, u32[]{:S(2)}) copy-start(bf16[512,512]{1,0:T(8,128)(2,1)} %copy-done.3) | copy-start | bytes 1572868
  71.0 20.5 %all-to-all-start.2 = ((bf16[16,32,1024]{2,1,0:T(8,128)(2,1)}), bf16[16,32,1024]{2,1,0:T(8,128)(2,1)S(1)}, u32[]{:S(2)}, u32[]{:S(2)}) async-start(bf16[16,32,1024]{2,1,0:T(8,128)(2,1)} %bitcast.66), calls=%async_computation.2 | async-start | bytes 2097152 | tf_op jit(solution)/shard_map/all_to_all | solution.py:13
  76.6 8.1 %collective-permute-start.6 = (bf16[128,1024]{1,0:T(8,128)(2,1)S(1)}, bf16[128,1024]{1,0:T(8,128)(2,1)S(1)}, u32[]{:S(2)}, u32[]{:S(2)}) collective-permute-start(bf16[128,1024]{1,0:T(8,128)(2,1)S(1)} %slice.89), channel_id=1, source_target_pairs={{0,1},{1,0},{2,3},{3,2},{4,5},{5,4},{6,7},{7,6},{8,9},{9,8},{10,11... | collective-permute-start | bytes 786440 | tf_op jit(solution)/shard_map/ppermute | solution.py:22
  84.8 6.6 %collective-permute-start.7 = (bf16[64,1024]{1,0:T(8,128)(2,1)S(1)}, bf16[64,1024]{1,0:T(8,128)(2,1)S(1)}, u32[]{:S(2)}, u32[]{:S(2)}) collective-permute-start(bf16[64,1024]{1,0:T(8,128)(2,1)S(1)} %slice.90), channel_id=1, source_target_pairs={{0,2},{2,0},{1,3},{3,1},{4,6},{6,4},{5,7},{7,5},{8,10},{10,8},{9,1... | collective-permute-start | bytes 393224 | tf_op jit(solution)/shard_map/ppermute | solution.py:22
  102.8 15.8 %all-to-all-start.4 = ((bf16[16,24,512]{2,1,0:T(8,128)(2,1)}), bf16[16,24,512]{2,1,0:T(8,128)(2,1)S(1)}, u32[]{:S(2)}, u32[]{:S(2)}) async-start(bf16[16,24,512]{2,1,0:T(8,128)(2,1)} %bitcast.26), calls=%async_computation.4 | async-start | bytes 786432 | tf_op jit(solution)/shard_map/all_to_all | solution.py:13
  143.7 6.5 %copy-start.1 = (bf16[16,1024]{1,0:T(8,128)(2,1)S(1)}, bf16[16,1024]{1,0:T(8,128)(2,1)}, u32[]{:S(2)}) copy-start(bf16[16,1024]{1,0:T(8,128)(2,1)} %param.7) | copy-start | bytes 98308
  144.5 13.2 %all-to-all-start.6 = ((bf16[16,24,512]{2,1,0:T(8,128)(2,1)}), bf16[16,24,512]{2,1,0:T(8,128)(2,1)S(1)}, u32[]{:S(2)}, u32[]{:S(2)}) async-start(bf16[16,24,512]{2,1,0:T(8,128)(2,1)} %broadcast_in_dim.30), calls=%async_computation.6 | async-start | bytes 786432 | tf_op jit(solution)/shard_map/all_to_all | solution.py:13

commit v5 on v4

--- a/solution.py
+++ b/solution.py
@@ -46,10 +46,10 @@
     partial_value = jnp.dot(features, proj_weight, preferred_element_type=F32).astype(BF)
     parts = partial_value.reshape(nx, own_rows, emb)
     half_embed = lax.dynamic_index_in_dim(parts, x, axis=0, keepdims=False).astype(F32)
-    for step in (2, 1, 3):
-        ring = [(i, (i + step) % nx) for i in range(nx)]
-        away = lax.dynamic_index_in_dim(parts, (x + step) % nx, axis=0, keepdims=False)
-        half_embed = half_embed + lax.ppermute(away, "x", ring).astype(F32)
+    for bit in (2, 1, 3):
+        pairs = [(i, i ^ bit) for i in range(nx)]
+        away = lax.dynamic_index_in_dim(parts, x ^ bit, axis=0, keepdims=False)
+        half_embed = half_embed + lax.ppermute(away, "x", pairs).astype(F32)
 
     text_value = text_embed.astype(F32)
     text_inverse = lax.rsqrt(jnp.sum(text_value * text_value, axis=1, keepdims=True) + 1e-06)

time: 160 us -> 162 us (1.012)
  waiting for transfers between devices: 28 us -> 31 us
  starting transfers between devices: 79.1 us -> 76.8 us
    ppermute x5, waiting for transfers between devices: 7.27 us -> 9.1 us  [flip(): return lax.ppermute(value, axis, [(0, 1), (1, 0)])]
    all_to_all x5, waiting for transfers between devices: 17 us -> 18.8 us  [exchange(): return lax.all_to_all(value, axes, 0, 0, tiled=False)]
  transfers between devices with their start and end apart: 13 -> 13, of which waited for: 8 -> 9; matrix products, arithmetic and copies ran while one was open for 4% -> 4% of each run, Pallas kernels for 0% -> 0%
where the time goes in v5:
time: 162 us; the launch traced here: 161 us
  starting transfers between devices  76.8 us (47%)
  blocking collectives  35 us (22%)
  waiting for transfers between devices  31 us (19%)
  other arithmetic  6.94 us (4%)
  matrix products  5.51 us (3%)
  local copies, waits for them, and re-layouts  2.89 us (2%)
  between operations  2.29 us (1%)
    all_to_all x5, starting transfers between devices, exchange(): return lax.all_to_all(value, axes, 0, 0, tiled=False)  36.7 us
    all_to_all x2, blocking collectives, exchange(): return lax.all_to_all(value, axes, 0, 0, tiled=False)  35 us
    ppermute x5, starting transfers between devices, flip(): return lax.ppermute(value, axis, [(0, 1), (1, 0)])  30.8 us
    all_to_all x5, waiting for transfers between devices, exchange(): return lax.all_to_all(value, axes, 0, 0, tiled=False)  18.8 us
    ppermute x3, starting transfers between devices, shards(): half_embed = half_embed + lax.ppermute(away, 'x', pairs).astype(F32)  9.34 us
    ppermute x5, waiting for transfers between devices, flip(): return lax.ppermute(value, axis, [(0, 1), (1, 0)])  9.1 us
  transfers between devices with their start and end apart: 13, of which 9 were waited for; matrix products, arithmetic and copies ran while one was open for 4% of the time, Pallas kernels for 0%

profile of v5, /device:TPU:1, one launch (start us, length us, event | category | flops | bytes accessed | tf_op | source)
XLA Modules:
  0.0 160.5 jit_solution(9707084300134168547)
XLA Ops:
  3.2 15.6 %all-to-all-start.1 = ((bf16[8,16,1024]{2,1,0:T(8,128)(2,1)}), bf16[8,16,1024]{2,1,0:T(8,128)(2,1)S(1)}, u32[]{:S(2)}, u32[]{:S(2)}) async-start(bf16[8,16,1024]{2,1,0:T(8,128)(2,1)} %broadcast_in_dim.25), calls=%async_computation.1 | async-start | bytes 524288 | tf_op jit(solution)/shard_map/all_to_all | solution.py:13
  19.9 4.6 %collective-permute-start = (bf16[32,1024]{1,0:T(8,128)(2,1)S(1)}, bf16[32,1024]{1,0:T(8,128)(2,1)S(1)}, u32[]{:S(2)}, u32[]{:S(2)}) collective-permute-start(bf16[32,1024]{1,0:T(8,128)(2,1)S(1)} %get-tuple-element.13), channel_id=1, source_target_pairs={{0,128},{64,192},{128,0},{192,64},{1,129},{65,193},{129,1},{193,65... | collective-permute-start | bytes 196616 | tf_op jit(solution)/shard_map/ppermute | solution.py:52
  24.5 2.8 %collective-permute-start.2 = (bf16[32,1024]{1,0:T(8,128)(2,1)S(1)}, bf16[32,1024]{1,0:T(8,128)(2,1)S(1)}, u32[]{:S(2)}, u32[]{:S(2)}) collective-permute-start(bf16[32,1024]{1,0:T(8,128)(2,1)S(1)} %get-tuple-element.14), channel_id=1, source_target_pairs={{0,192},{64,128},{128,64},{192,0},{1,193},{65,129},{129,65},{193,1... | collective-permute-start | bytes 196616 | tf_op jit(solution)/shard_map/ppermute | solution.py:52
  27.3 1.9 %collective-permute-start.1 = (bf16[32,1024]{1,0:T(8,128)(2,1)S(1)}, bf16[32,1024]{1,0:T(8,128)(2,1)S(1)}, u32[]{:S(2)}, u32[]{:S(2)}) collective-permute-start(bf16[32,1024]{1,0:T(8,128)(2,1)S(1)} %get-tuple-element.15), channel_id=1, source_target_pairs={{0,64},{64,0},{128,192},{192,128},{1,65},{65,1},{129,193},{193,129... | collective-permute-start | bytes 196616 | tf_op jit(solution)/shard_map/ppermute | solution.py:52
  29.5 1.6 collective-permute-done.2
  31.1 1.6 collective-permute-done.1
  32.7 12.1 %collective-permute-start.3 = (bf16[32,1024]{1,0:T(8,128)(2,1)S(1)}, bf16[32,1024]{1,0:T(8,128)(2,1)S(1)}, u32[]{:S(2)}, u32[]{:S(2)}) collective-permute-start(bf16[32,1024]{1,0:T(8,128)(2,1)S(1)} %fusion.26), channel_id=1, source_target_pairs={{0,256},{256,0},{1,257},{257,1},{2,258},{258,2},{3,259},{259,3},{4... | collective-permute-start | bytes 196616 | tf_op jit(solution)/shard_map/ppermute | solution.py:22
  46.2 1.9 %collective-permute-done.3 = bf16[32,1024]{1,0:T(8,128)(2,1)S(1)} collective-permute-done((bf16[32,1024]{1,0:T(8,128)(2,1)S(1)}, bf16[32,1024]{1,0:T(8,128)(2,1)S(1)}, u32[]{:S(2)}, u32[]{:S(2)}) %collective-permute-start.3) | collective-permute-done | bytes 65568 | tf_op jit(solution)/shard_map/ppermute | solution.py:22
  48.3 2.6 %collective-permute-start.4 = (bf16[2,1,64,1024]{3,2,1,0:T(8,128)(2,1)S(1)}, bf16[2,1,64,1024]{3,2,1,0:T(8,128)(2,1)S(1)}, u32[]{:S(2)}, u32[]{:S(2)}) collective-permute-start(bf16[2,1,64,1024]{3,2,1,0:T(8,128)(2,1)S(1)} %maximum_bitcast_fusion.1), channel_id=1, source_target_pairs={{0,2},{2,0},{1,3},{3,1},{4,6},{6,4},{5,7},{7,5},{8,10},{10,8},{9,1... | collective-permute-start | bytes 786440 | tf_op jit(solution)/shard_map/ppermute | solution.py:22
  52.1 5.6 %all-to-all-start = ((bf16[16,32,1024]{2,1,0:T(8,128)(2,1)}), bf16[16,32,1024]{2,1,0:T(8,128)(2,1)S(1)}, u32[]{:S(2)}, u32[]{:S(2)}) async-start(bf16[16,32,1024]{2,1,0:T(8,128)(2,1)} %broadcast_in_dim.24), calls=%async_computation | async-start | bytes 2097152 | tf_op jit(solution)/shard_map/all_to_all | solution.py:13
  57.8 6.7 %collective-permute-start.5 = (bf16[2,1,2,64,1024]{4,3,2,1,0:T(8,128)(2,1)S(1)}, bf16[2,1,2,64,1024]{4,3,2,1,0:T(8,128)(2,1)}, u32[]{:S(2)}, u32[]{:S(2)}) collective-permute-start(bf16[2,1,2,64,1024]{4,3,2,1,0:T(8,128)(2,1)S(1)} %maximum_bitcast_fusion), channel_id=1, source_target_pairs={{0,1},{1,0},{2,3},{3,2},{4,5},{5,4},{6,7},{7,6},{8,9},{9,8},{10,11... | collective-permute-start | bytes 1572872 | tf_op jit(solution)/shard_map/ppermute | solution.py:22
  64.8 1.4 collective-permute-done.5
  67.3 3.8 %all-to-all-done = bf16[16,32,1024]{2,1,0:T(8,128)(2,1)S(1)} async-done(((bf16[16,32,1024]{2,1,0:T(8,128)(2,1)}), bf16[16,32,1024]{2,1,0:T(8,128)(2,1)S(1)}, u32[]{:S(2)}, u32[]{:S(2)}) %all-to-all-start) | async-done | bytes 1048608 | tf_op jit(solution)/shard_map/all_to_all | solution.py:13
  72.1 1.7 %convolution_convert_fusion = bf16[512,1024]{1,0:T(8,128)(2,1)} fusion(bf16[512,512]{1,0:T(8,128)(2,1)S(1)} %fusion.8, bf16[512,1024]{1,0:T(8,128)(2,1)S(1)} %bitcast.68), kind=kOutput, calls=%fused_computation.1 | convolution fusion | flops 537395200 | bytes 2621440 | tf_op jit(solution)/shard_map/dot_general | solution.py:102
  73.8 3.8 %all-to-all-start.2 = ((bf16[16,32,1024]{2,1,0:T(8,128)(2,1)}), bf16[16,32,1024]{2,1,0:T(8,128)(2,1)S(1)}, u32[]{:S(2)}, u32[]{:S(2)}) async-start(bf16[16,32,1024]{2,1,0:T(8,128)(2,1)} %bitcast.66), calls=%async_computation.2 | async-start | bytes 2097152 | tf_op jit(solution)/shard_map/all_to_all | solution.py:13
  78.1 7.5 %collective-permute-start.6 = (bf16[128,1024]{1,0:T(8,128)(2,1)S(1)}, bf16[128,1024]{1,0:T(8,128)(2,1)S(1)}, u32[]{:S(2)}, u32[]{:S(2)}) collective-permute-start(bf16[128,1024]{1,0:T(8,128)(2,1)S(1)} %slice.89), channel_id=1, source_target_pairs={{0,1},{1,0},{2,3},{3,2},{4,5},{5,4},{6,7},{7,6},{8,9},{9,8},{10,11... | collective-permute-start | bytes 786440 | tf_op jit(solution)/shard_map/ppermute | solution.py:22
  86.8 1.9 %collective-permute-start.7 = (bf16[64,1024]{1,0:T(8,128)(2,1)S(1)}, bf16[64,1024]{1,0:T(8,128)(2,1)S(1)}, u32[]{:S(2)}, u32[]{:S(2)}) collective-permute-start(bf16[64,1024]{1,0:T(8,128)(2,1)S(1)} %slice.90), channel_id=1, source_target_pairs={{0,2},{2,0},{1,3},{3,1},{4,6},{6,4},{5,7},{7,5},{8,10},{10,8},{9,1... | collective-permute-start | bytes 393224 | tf_op jit(solution)/shard_map/ppermute | solution.py:22
  88.7 4.7 %collective-permute-done.7 = bf16[64,1024]{1,0:T(8,128)(2,1)S(1)} collective-permute-done((bf16[64,1024]{1,0:T(8,128)(2,1)S(1)}, bf16[64,1024]{1,0:T(8,128)(2,1)S(1)}, u32[]{:S(2)}, u32[]{:S(2)}) %collective-permute-start.7) | collective-permute-done | bytes 131104 | tf_op jit(solution)/shard_map/ppermute | solution.py:22
  94.0 9.6 %all_to_all.35 = bf16[4,32,1024]{2,1,0:T(8,128)(2,1)S(1)} all-to-all(bf16[4,32,1024]{2,1,0:T(8,128)(2,1)S(1)} %broadcast_in_dim.28), channel_id=1, replica_groups=mesh['zh'=2,'x'=4,'y'=4,'zq'=4,'zp'=2,'c'=2] {'x'}, dimensions={0} | all-to-all | bytes 524288 | tf_op jit(solution)/shard_map/all_to_all | solution.py:13
  104.8 6.9 %all-to-all-start.4 = ((bf16[16,24,512]{2,1,0:T(8,128)(2,1)}), bf16[16,24,512]{2,1,0:T(8,128)(2,1)S(1)}, u32[]{:S(2)}, u32[]{:S(2)}) async-start(bf16[16,24,512]{2,1,0:T(8,128)(2,1)} %bitcast.26), calls=%async_computation.4 | async-start | bytes 786432 | tf_op jit(solution)/shard_map/all_to_all | solution.py:13
  111.8 8.4 %all-to-all-done.4 = bf16[16,24,512]{2,1,0:T(8,128)(2,1)S(1)} async-done(((bf16[16,24,512]{2,1,0:T(8,128)(2,1)}), bf16[16,24,512]{2,1,0:T(8,128)(2,1)S(1)}, u32[]{:S(2)}, u32[]{:S(2)}) %all-to-all-start.4) | async-done | bytes 393248 | tf_op jit(solution)/shard_map/all_to_all | solution.py:13
  120.3 25.4 %all_to_all.36 = bf16[4,56,512]{2,1,0:T(8,128)(2,1)S(1)} all-to-all(bf16[4,56,512]{2,1,0:T(8,128)(2,1)S(1)} %pad_maximum_fusion.3), channel_id=1, replica_groups=mesh['zh'=2,'x'=4,'y'=4,'zq'=4,'zp'=2,'c'=2] {'zq'}, dimensions={0} | all-to-all | bytes 458752 | tf_op jit(solution)/shard_map/all_to_all | solution.py:13
  146.5 4.8 %all-to-all-start.6 = ((bf16[16,24,512]{2,1,0:T(8,128)(2,1)}), bf16[16,24,512]{2,1,0:T(8,128)(2,1)S(1)}, u32[]{:S(2)}, u32[]{:S(2)}) async-start(bf16[16,24,512]{2,1,0:T(8,128)(2,1)} %broadcast_in_dim.30), calls=%async_computation.6 | async-start | bytes 786432 | tf_op jit(solution)/shard_map/all_to_all | solution.py:13
  153.0 6.7 %all-to-all-done.6 = bf16[16,24,512]{2,1,0:T(8,128)(2,1)S(1)} async-done(((bf16[16,24,512]{2,1,0:T(8,128)(2,1)}), bf16[16,24,512]{2,1,0:T(8,128)(2,1)S(1)}, u32[]{:S(2)}, u32[]{:S(2)}) %all-to-all-start.6) | async-done | bytes 393248 | tf_op jit(solution)/shard_map/all_to_all | solution.py:13
  (65 shorter events, 14.8 us)
Async XLA Ops:
  0.6 18.2 %copy-start = (bf16[192,1024]{1,0:T(8,128)(2,1)S(1)}, bf16[192,1024]{1,0:T(8,128)(2,1)}, u32[]{:S(2)}) copy-start(bf16[192,1024]{1,0:T(8,128)(2,1)} %param.6) | copy-start | bytes 1179652
  3.2 45.1 %all-to-all-start.1 = ((bf16[8,16,1024]{2,1,0:T(8,128)(2,1)}), bf16[8,16,1024]{2,1,0:T(8,128)(2,1)S(1)}, u32[]{:S(2)}, u32[]{:S(2)}) async-start(bf16[8,16,1024]{2,1,0:T(8,128)(2,1)} %broadcast_in_dim.25), calls=%async_computation.1 | async-start | bytes 524288 | tf_op jit(solution)/shard_map/all_to_all | solution.py:13
  19.9 9.6 %collective-permute-start = (bf16[32,1024]{1,0:T(8,128)(2,1)S(1)}, bf16[32,1024]{1,0:T(8,128)(2,1)S(1)}, u32[]{:S(2)}, u32[]{:S(2)}) collective-permute-start(bf16[32,1024]{1,0:T(8,128)(2,1)S(1)} %get-tuple-element.13), channel_id=1, source_target_pairs={{0,128},{64,192},{128,0},{192,64},{1,129},{65,193},{129,1},{193,65... | collective-permute-start | bytes 196616 | tf_op jit(solution)/shard_map/ppermute | solution.py:52
  24.5 6.5 %collective-permute-start.2 = (bf16[32,1024]{1,0:T(8,128)(2,1)S(1)}, bf16[32,1024]{1,0:T(8,128)(2,1)S(1)}, u32[]{:S(2)}, u32[]{:S(2)}) collective-permute-start(bf16[32,1024]{1,0:T(8,128)(2,1)S(1)} %get-tuple-element.14), channel_id=1, source_target_pairs={{0,192},{64,128},{128,64},{192,0},{1,193},{65,129},{129,65},{193,1... | collective-permute-start | bytes 196616 | tf_op jit(solution)/shard_map/ppermute | solution.py:52
  27.3 5.3 %collective-permute-start.1 = (bf16[32,1024]{1,0:T(8,128)(2,1)S(1)}, bf16[32,1024]{1,0:T(8,128)(2,1)S(1)}, u32[]{:S(2)}, u32[]{:S(2)}) collective-permute-start(bf16[32,1024]{1,0:T(8,128)(2,1)S(1)} %get-tuple-element.15), channel_id=1, source_target_pairs={{0,64},{64,0},{128,192},{192,128},{1,65},{65,1},{129,193},{193,129... | collective-permute-start | bytes 196616 | tf_op jit(solution)/shard_map/ppermute | solution.py:52
  32.7 15.4 %collective-permute-start.3 = (bf16[32,1024]{1,0:T(8,128)(2,1)S(1)}, bf16[32,1024]{1,0:T(8,128)(2,1)S(1)}, u32[]{:S(2)}, u32[]{:S(2)}) collective-permute-start(bf16[32,1024]{1,0:T(8,128)(2,1)S(1)} %fusion.26), channel_id=1, source_target_pairs={{0,256},{256,0},{1,257},{257,1},{2,258},{258,2},{3,259},{259,3},{4... | collective-permute-start | bytes 196616 | tf_op jit(solution)/shard_map/ppermute | solution.py:22
  48.3 9.5 %collective-permute-start.4 = (bf16[2,1,64,1024]{3,2,1,0:T(8,128)(2,1)S(1)}, bf16[2,1,64,1024]{3,2,1,0:T(8,128)(2,1)S(1)}, u32[]{:S(2)}, u32[]{:S(2)}) collective-permute-start(bf16[2,1,64,1024]{3,2,1,0:T(8,128)(2,1)S(1)} %maximum_bitcast_fusion.1), channel_id=1, source_target_pairs={{0,2},{2,0},{1,3},{3,1},{4,6},{6,4},{5,7},{7,5},{8,10},{10,8},{9,1... | collective-permute-start | bytes 786440 | tf_op jit(solution)/shard_map/ppermute | solution.py:22
  52.1 18.9 %all-to-all-start = ((bf16[16,32,1024]{2,1,0:T(8,128)(2,1)}), bf16[16,32,1024]{2,1,0:T(8,128)(2,1)S(1)}, u32[]{:S(2)}, u32[]{:S(2)}) async-start(bf16[16,32,1024]{2,1,0:T(8,128)(2,1)} %broadcast_in_dim.24), calls=%async_computation | async-start | bytes 2097152 | tf_op jit(solution)/shard_map/all_to_all | solution.py:13
  57.8 8.3 %collective-permute-start.5 = (bf16[2,1,2,64,1024]{4,3,2,1,0:T(8,128)(2,1)S(1)}, bf16[2,1,2,64,1024]{4,3,2,1,0:T(8,128)(2,1)}, u32[]{:S(2)}, u32[]{:S(2)}) collective-permute-start(bf16[2,1,2,64,1024]{4,3,2,1,0:T(8,128)(2,1)S(1)} %maximum_bitcast_fusion), channel_id=1, source_target_pairs={{0,1},{1,0},{2,3},{3,2},{4,5},{5,4},{6,7},{7,6},{8,9},{9,8},{10,11... | collective-permute-start | bytes 1572872 | tf_op jit(solution)/shard_map/ppermute | solution.py:22
  72.1 1.7 %copy-start.3 = (bf16[512,512]{1,0:T(8,128)(2,1)}, bf16[512,512]{1,0:T(8,128)(2,1)S(1)}, u32[]{:S(2)}) copy-start(bf16[512,512]{1,0:T(8,128)(2,1)S(1)} %fusion.8) | copy-start | bytes 1572868
  73.8 3.8 %copy-start.4 = (bf16[512,512]{1,0:T(8,128)(2,1)S(1)}, bf16[512,512]{1,0:T(8,128)(2,1)}, u32[]{:S(2)}) copy-start(bf16[512,512]{1,0:T(8,128)(2,1)} %copy-done.3) | copy-start | bytes 1572868
  73.8 19.7 %all-to-all-start.2 = ((bf16[16,32,1024]{2,1,0:T(8,128)(2,1)}), bf16[16,32,1024]{2,1,0:T(8,128)(2,1)S(1)}, u32[]{:S(2)}, u32[]{:S(2)}) async-start(bf16[16,32,1024]{2,1,0:T(8,128)(2,1)} %bitcast.66), calls=%async_computation.2 | async-start | bytes 2097152 | tf_op jit(solution)/shard_map/all_to_all | solution.py:13
  78.1 8.6 %collective-permute-start.6 = (bf16[128,1024]{1,0:T(8,128)(2,1)S(1)}, bf16[128,1024]{1,0:T(8,128)(2,1)S(1)}, u32[]{:S(2)}, u32[]{:S(2)}) collective-permute-start(bf16[128,1024]{1,0:T(8,128)(2,1)S(1)} %slice.89), channel_id=1, source_target_pairs={{0,1},{1,0},{2,3},{3,2},{4,5},{5,4},{6,7},{7,6},{8,9},{9,8},{10,11... | collective-permute-start | bytes 786440 | tf_op jit(solution)/shard_map/ppermute | solution.py:22
  86.8 6.6 %collective-permute-start.7 = (bf16[64,1024]{1,0:T(8,128)(2,1)S(1)}, bf16[64,1024]{1,0:T(8,128)(2,1)S(1)}, u32[]{:S(2)}, u32[]{:S(2)}) collective-permute-start(bf16[64,1024]{1,0:T(8,128)(2,1)S(1)} %slice.90), channel_id=1, source_target_pairs={{0,2},{2,0},{1,3},{3,1},{4,6},{6,4},{5,7},{7,5},{8,10},{10,8},{9,1... | collective-permute-start | bytes 393224 | tf_op jit(solution)/shard_map/ppermute | solution.py:22
  93.5 10.2 %copy-start.2 = (bf16[128,192]{0,1:T(8,128)(2,1)S(1)}, bf16[128,192]{0,1:T(8,128)(2,1)}, u32[]{:S(2)}) copy-start(bf16[128,192]{0,1:T(8,128)(2,1)} %param.5) | copy-start | bytes 147460
  104.8 15.3 %all-to-all-start.4 = ((bf16[16,24,512]{2,1,0:T(8,128)(2,1)}), bf16[16,24,512]{2,1,0:T(8,128)(2,1)S(1)}, u32[]{:S(2)}, u32[]{:S(2)}) async-start(bf16[16,24,512]{2,1,0:T(8,128)(2,1)} %bitcast.26), calls=%async_computation.4 | async-start | bytes 786432 | tf_op jit(solution)/shard_map/all_to_all | solution.py:13
  145.7 6.5 %copy-start.1 = (bf16[16,1024]{1,0:T(8,128)(2,1)S(1)}, bf16[16,1024]{1,0:T(8,128)(2,1)}, u32[]{:S(2)}) copy-start(bf16[16,1024]{1,0:T(8,128)(2,1)} %param.7) | copy-start | bytes 98308
  146.5 13.2 %all-to-all-start.6 = ((bf16[16,24,512]{2,1,0:T(8,128)(2,1)}), bf16[16,24,512]{2,1,0:T(8,128)(2,1)S(1)}, u32[]{:S(2)}, u32[]{:S(2)}) async-start(bf16[16,24,512]{2,1,0:T(8,128)(2,1)} %broadcast_in_dim.30), calls=%async_computation.6 | async-start | bytes 786432 | tf_op jit(solution)/shard_map/all_to_all | solution.py:13

commit v6 on v4

--- a/solution.py
+++ b/solution.py
@@ -114,38 +114,25 @@
     embed_rows = unit_backward(unit_grad, unit_full, image_inverse).astype(BF)
     embed_grad = gather(embed_rows, "x").reshape(block_rows, emb)
 
-    width = emb // 2
-    weight_part = jnp.stack(
-        [
-            lax.dot_general(
-                features, half, (((0,), (0,)), ((), ())), preferred_element_type=F32
-            ).astype(BF)
-            for half in (embed_grad[:, :width], embed_grad[:, width:])
-        ]
-    )
+    weight_part = lax.dot_general(
+        features, embed_grad, (((0,), (0,)), ((), ())), preferred_element_type=F32
+    ).astype(BF)
     image_grad = lax.dot_general(
         embed_grad, proj_weight, (((1,), (1,)), ((), ())), preferred_element_type=F32
     ).astype(BF)
 
     near = ("zp", "y", "c")
-    weight_rows = features.shape[1] // (ny * 2)
-    weight_parts = exchange(weight_part.reshape(ny * 4, weight_rows, width), near)
+    weight_rows = features.shape[1] // (ny * 4)
+    weight_parts = exchange(weight_part.reshape(ny * 4, weight_rows, emb), near)
     weight_sum = jnp.sum(weight_parts.astype(F32), axis=0).astype(BF)
     line_sent = jnp.concatenate(
-        [
-            jnp.broadcast_to(weight_sum[None], (nq, weight_rows, width)),
-            text_home[:, :, :width],
-            text_home[:, :, width:],
-        ],
-        axis=1,
+        [text_home, jnp.broadcast_to(weight_sum[None], (nq,) + weight_sum.shape)], axis=1
     )
     line_sum = jnp.sum(exchange(line_sent, "zq").astype(F32), axis=0)
-    weight_own = line_sum[:weight_rows].astype(BF)
-    weight_grad = gather(weight_own, near).reshape(2, features.shape[1], width)
-    weight_grad = jnp.concatenate([weight_grad[0], weight_grad[1]], axis=1)
+    weight_own = line_sum[text_rows:].astype(BF)
+    weight_grad = gather(weight_own, near).reshape(weight_part.shape)
 
-    text_sum = line_sum[weight_rows:]
-    text_unit_grad = jnp.concatenate([text_sum[:text_rows], text_sum[text_rows:]], axis=1)
+    text_unit_grad = line_sum[:text_rows]
     text_grad = unit_backward(text_unit_grad, text_full, text_inverse).astype(BF)
     return (image_grad, weight_grad, text_grad)
 

time: 160 us -> 163 us (1.019)
  blocking collectives: 34.7 us -> 53.3 us
  starting transfers between devices: 79.1 us -> 71.5 us
  waiting for transfers between devices: 28 us -> 21.1 us
    all_to_all x2 -> x3, blocking collectives: 34.7 us -> 53.3 us  [exchange(): return lax.all_to_all(value, axes, 0, 0, tiled=False)]
    all_to_all x5 -> x4, starting transfers between devices: 37.8 us -> 30.2 us  [exchange(): return lax.all_to_all(value, axes, 0, 0, tiled=False)]
    all_to_all x5 -> x4, waiting for transfers between devices: 17 us -> 10 us  [exchange(): return lax.all_to_all(value, axes, 0, 0, tiled=False)]
  transfers between devices with their start and end apart: 13 -> 12, of which waited for: 8 -> 7; matrix products, arithmetic and copies ran while one was open for 4% -> 4% of each run, Pallas kernels for 0% -> 0%
where the time goes in v6:
time: 163 us; the launch traced here: 162 us
  starting transfers between devices  71.5 us (44%)
  blocking collectives  53.3 us (33%)
  waiting for transfers between devices  21.1 us (13%)
  other arithmetic  5.42 us (3%)
  matrix products  4.57 us (3%)
  local copies, waits for them, and re-layouts  3.86 us (2%)
  between operations  2.28 us (1%)
    all_to_all x3, blocking collectives, exchange(): return lax.all_to_all(value, axes, 0, 0, tiled=False)  53.3 us
    ppermute x5, starting transfers between devices, flip(): return lax.ppermute(value, axis, [(0, 1), (1, 0)])  31.3 us
    all_to_all x4, starting transfers between devices, exchange(): return lax.all_to_all(value, axes, 0, 0, tiled=False)  30.2 us
    all_to_all x4, waiting for transfers between devices, exchange(): return lax.all_to_all(value, axes, 0, 0, tiled=False)  10 us
    ppermute x3, starting transfers between devices, shards(): half_embed = half_embed + lax.ppermute(away, 'x', ring).astype(F32)  9.93 us
    ppermute x5, waiting for transfers between devices, flip(): return lax.ppermute(value, axis, [(0, 1), (1, 0)])  7.27 us
    ppermute x3, waiting for transfers between devices, shards(): half_embed = half_embed + lax.ppermute(away, 'x', ring).astype(F32)  3.75 us
  transfers between devices with their start and end apart: 12, of which 7 were waited for; matrix products, arithmetic and copies ran while one was open for 4% of the time, Pallas kernels for 0%

profile of v6, /device:TPU:1, one launch (start us, length us, event | category | flops | bytes accessed | tf_op | source)
XLA Modules:
  0.0 161.9 jit_solution(14343651654018344609)
XLA Ops:
  3.2 15.6 %all-to-all-start.1 = ((bf16[8,16,1024]{2,1,0:T(8,128)(2,1)}), bf16[8,16,1024]{2,1,0:T(8,128)(2,1)S(1)}, u32[]{:S(2)}, u32[]{:S(2)}) async-start(bf16[8,16,1024]{2,1,0:T(8,128)(2,1)} %broadcast_in_dim.25), calls=%async_computation.1 | async-start | bytes 524288 | tf_op jit(solution)/shard_map/all_to_all | solution.py:13
  19.1 4.7 %collective-permute-start = (bf16[32,1024]{1,0:T(8,128)(2,1)S(1)}, bf16[32,1024]{1,0:T(8,128)(2,1)S(1)}, u32[]{:S(2)}, u32[]{:S(2)}) collective-permute-start(bf16[32,1024]{1,0:T(8,128)(2,1)S(1)} %get-tuple-element.11), channel_id=1, source_target_pairs={{0,128},{64,192},{128,0},{192,64},{1,129},{65,193},{129,1},{193,65... | collective-permute-start | bytes 196616 | tf_op jit(solution)/shard_map/ppermute | solution.py:52
  23.8 2.8 %collective-permute-start.2 = (bf16[32,1024]{1,0:T(8,128)(2,1)S(1)}, bf16[32,1024]{1,0:T(8,128)(2,1)S(1)}, u32[]{:S(2)}, u32[]{:S(2)}) collective-permute-start(bf16[32,1024]{1,0:T(8,128)(2,1)S(1)} %get-tuple-element.12), channel_id=1, source_target_pairs={{0,192},{64,0},{128,64},{192,128},{1,193},{65,1},{129,65},{193,129... | collective-permute-start | bytes 196616 | tf_op jit(solution)/shard_map/ppermute | solution.py:52
  26.5 2.5 %collective-permute-start.1 = (bf16[32,1024]{1,0:T(8,128)(2,1)S(1)}, bf16[32,1024]{1,0:T(8,128)(2,1)S(1)}, u32[]{:S(2)}, u32[]{:S(2)}) collective-permute-start(bf16[32,1024]{1,0:T(8,128)(2,1)S(1)} %get-tuple-element.13), channel_id=1, source_target_pairs={{0,64},{64,128},{128,192},{192,0},{1,65},{65,129},{129,193},{193,1... | collective-permute-start | bytes 196616 | tf_op jit(solution)/shard_map/ppermute | solution.py:52
  29.3 3.7 %collective-permute-done.1 = bf16[32,1024]{1,0:T(8,128)(2,1)S(1)} collective-permute-done((bf16[32,1024]{1,0:T(8,128)(2,1)S(1)}, bf16[32,1024]{1,0:T(8,128)(2,1)S(1)}, u32[]{:S(2)}, u32[]{:S(2)}) %collective-permute-start.1) | collective-permute-done | bytes 65568 | tf_op jit(solution)/shard_map/ppermute | solution.py:52
  33.1 11.8 %collective-permute-start.3 = (bf16[32,1024]{1,0:T(8,128)(2,1)S(1)}, bf16[32,1024]{1,0:T(8,128)(2,1)S(1)}, u32[]{:S(2)}, u32[]{:S(2)}) collective-permute-start(bf16[32,1024]{1,0:T(8,128)(2,1)S(1)} %fusion.23), channel_id=1, source_target_pairs={{0,256},{256,0},{1,257},{257,1},{2,258},{258,2},{3,259},{259,3},{4... | collective-permute-start | bytes 196616 | tf_op jit(solution)/shard_map/ppermute | solution.py:22
  47.3 2.6 %collective-permute-start.4 = (bf16[2,1,64,1024]{3,2,1,0:T(8,128)(2,1)S(1)}, bf16[2,1,64,1024]{3,2,1,0:T(8,128)(2,1)S(1)}, u32[]{:S(2)}, u32[]{:S(2)}) collective-permute-start(bf16[2,1,64,1024]{3,2,1,0:T(8,128)(2,1)S(1)} %maximum_bitcast_fusion.1), channel_id=1, source_target_pairs={{0,2},{2,0},{1,3},{3,1},{4,6},{6,4},{5,7},{7,5},{8,10},{10,8},{9,1... | collective-permute-start | bytes 786440 | tf_op jit(solution)/shard_map/ppermute | solution.py:22
  50.0 1.1 broadcast_in_dim.24
  51.0 4.9 %all-to-all-start = ((bf16[16,32,1024]{2,1,0:T(8,128)(2,1)}), bf16[16,32,1024]{2,1,0:T(8,128)(2,1)S(1)}, u32[]{:S(2)}, u32[]{:S(2)}) async-start(bf16[16,32,1024]{2,1,0:T(8,128)(2,1)} %broadcast_in_dim.24), calls=%async_computation | async-start | bytes 2097152 | tf_op jit(solution)/shard_map/all_to_all | solution.py:13
  56.1 7.4 %collective-permute-start.5 = (bf16[2,1,2,64,1024]{4,3,2,1,0:T(8,128)(2,1)S(1)}, bf16[2,1,2,64,1024]{4,3,2,1,0:T(8,128)(2,1)}, u32[]{:S(2)}, u32[]{:S(2)}) collective-permute-start(bf16[2,1,2,64,1024]{4,3,2,1,0:T(8,128)(2,1)S(1)} %maximum_bitcast_fusion), channel_id=1, source_target_pairs={{0,1},{1,0},{2,3},{3,2},{4,5},{5,4},{6,7},{7,6},{8,9},{9,8},{10,11... | collective-permute-start | bytes 1572872 | tf_op jit(solution)/shard_map/ppermute | solution.py:22
  63.8 1.4 collective-permute-done.5
  65.2 1.1 pad_maximum_fusion
  66.3 1.9 %all-to-all-done = bf16[16,32,1024]{2,1,0:T(8,128)(2,1)S(1)} async-done(((bf16[16,32,1024]{2,1,0:T(8,128)(2,1)}), bf16[16,32,1024]{2,1,0:T(8,128)(2,1)S(1)}, u32[]{:S(2)}, u32[]{:S(2)}) %all-to-all-start) | async-done | bytes 1048608 | tf_op jit(solution)/shard_map/all_to_all | solution.py:13
  69.3 1.7 %convolution_convert_fusion = bf16[512,1024]{1,0:T(8,128)(2,1)} fusion(bf16[512,512]{1,0:T(8,128)(2,1)S(1)} %fusion.8, bf16[512,1024]{1,0:T(8,128)(2,1)S(1)} %bitcast.58), kind=kOutput, calls=%fused_computation.1 | convolution fusion | flops 537395200 | bytes 2621440 | tf_op jit(solution)/shard_map/dot_general | solution.py:102
  71.0 5.1 %all-to-all-start.2 = ((bf16[16,32,1024]{2,1,0:T(8,128)(2,1)}), bf16[16,32,1024]{2,1,0:T(8,128)(2,1)S(1)}, u32[]{:S(2)}, u32[]{:S(2)}) async-start(bf16[16,32,1024]{2,1,0:T(8,128)(2,1)} %bitcast.56), calls=%async_computation.2 | async-start | bytes 2097152 | tf_op jit(solution)/shard_map/all_to_all | solution.py:13
  76.6 7.0 %collective-permute-start.6 = (bf16[128,1024]{1,0:T(8,128)(2,1)S(1)}, bf16[128,1024]{1,0:T(8,128)(2,1)S(1)}, u32[]{:S(2)}, u32[]{:S(2)}) collective-permute-start(bf16[128,1024]{1,0:T(8,128)(2,1)S(1)} %slice.49), channel_id=1, source_target_pairs={{0,1},{1,0},{2,3},{3,2},{4,5},{5,4},{6,7},{7,6},{8,9},{9,8},{10,11... | collective-permute-start | bytes 786440 | tf_op jit(solution)/shard_map/ppermute | solution.py:22
  83.6 1.1 collective-permute-done.6
  84.8 2.6 %collective-permute-start.7 = (bf16[64,1024]{1,0:T(8,128)(2,1)S(1)}, bf16[64,1024]{1,0:T(8,128)(2,1)S(1)}, u32[]{:S(2)}, u32[]{:S(2)}) collective-permute-start(bf16[64,1024]{1,0:T(8,128)(2,1)S(1)} %slice.50), channel_id=1, source_target_pairs={{0,2},{2,0},{1,3},{3,1},{4,6},{6,4},{5,7},{7,5},{8,10},{10,8},{9,1... | collective-permute-start | bytes 393224 | tf_op jit(solution)/shard_map/ppermute | solution.py:22
  87.5 4.0 %collective-permute-done.7 = bf16[64,1024]{1,0:T(8,128)(2,1)S(1)} collective-permute-done((bf16[64,1024]{1,0:T(8,128)(2,1)S(1)}, bf16[64,1024]{1,0:T(8,128)(2,1)S(1)}, u32[]{:S(2)}, u32[]{:S(2)}) %collective-permute-start.7) | collective-permute-done | bytes 131104 | tf_op jit(solution)/shard_map/ppermute | solution.py:22
  92.0 9.6 %all_to_all.35 = bf16[4,32,1024]{2,1,0:T(8,128)(2,1)S(1)} all-to-all(bf16[4,32,1024]{2,1,0:T(8,128)(2,1)S(1)} %broadcast_in_dim.28), channel_id=1, replica_groups=mesh['zh'=2,'x'=4,'y'=4,'zq'=4,'zp'=2,'c'=2] {'x'}, dimensions={0} | all-to-all | bytes 524288 | tf_op jit(solution)/shard_map/all_to_all | solution.py:13
  102.0 17.0 %all_to_all.36 = bf16[16,12,1024]{2,1,0:T(8,128)(2,1)S(1)} all-to-all(bf16[16,12,1024]{2,1,0:T(8,128)(2,1)S(1)} %reshape.185), channel_id=1, replica_groups=mesh['zh'=2,'x'=4,'y'=4,'zq'=4,'zp'=2,'c'=2] {'zp','y','c'}, dimensions={0} | all-to-all | bytes 786432 | tf_op jit(solution)/shard_map/all_to_all | solution.py:13
  119.1 26.7 %all_to_all.37 = bf16[4,28,1024]{2,1,0:T(8,128)(2,1)S(1)} all-to-all(bf16[4,28,1024]{2,1,0:T(8,128)(2,1)S(1)} %pad_maximum_fusion.1), channel_id=1, replica_groups=mesh['zh'=2,'x'=4,'y'=4,'zq'=4,'zp'=2,'c'=2] {'zq'}, dimensions={0} | all-to-all | bytes 458752 | tf_op jit(solution)/shard_map/all_to_all | solution.py:13
  146.7 4.5 %all-to-all-start.6 = ((bf16[16,12,1024]{2,1,0:T(8,128)(2,1)}), bf16[16,12,1024]{2,1,0:T(8,128)(2,1)S(1)}, u32[]{:S(2)}, u32[]{:S(2)}) async-start(bf16[16,12,1024]{2,1,0:T(8,128)(2,1)} %broadcast_in_dim.30), calls=%async_computation.6 | async-start | bytes 1048576 | tf_op jit(solution)/shard_map/all_to_all | solution.py:13
  153.0 8.1 %all-to-all-done.6 = bf16[16,12,1024]{2,1,0:T(8,128)(2,1)S(1)} async-done(((bf16[16,12,1024]{2,1,0:T(8,128)(2,1)}), bf16[16,12,1024]{2,1,0:T(8,128)(2,1)S(1)}, u32[]{:S(2)}, u32[]{:S(2)}) %all-to-all-start.6) | async-done | bytes 393248 | tf_op jit(solution)/shard_map/all_to_all | solution.py:13
  (60 shorter events, 10.7 us)
Async XLA Ops:
  0.6 18.2 %copy-start = (bf16[192,1024]{1,0:T(8,128)(2,1)S(1)}, bf16[192,1024]{1,0:T(8,128)(2,1)}, u32[]{:S(2)}) copy-start(bf16[192,1024]{1,0:T(8,128)(2,1)} %param.6) | copy-start | bytes 1179652
  0.6 18.2 %copy-start.2 = (bf16[128,192]{0,1:T(8,128)(2,1)S(1)}, bf16[128,192]{0,1:T(8,128)(2,1)}, u32[]{:S(2)}) copy-start(bf16[128,192]{0,1:T(8,128)(2,1)} %param.5) | copy-start | bytes 147460
  3.2 44.1 %all-to-all-start.1 = ((bf16[8,16,1024]{2,1,0:T(8,128)(2,1)}), bf16[8,16,1024]{2,1,0:T(8,128)(2,1)S(1)}, u32[]{:S(2)}, u32[]{:S(2)}) async-start(bf16[8,16,1024]{2,1,0:T(8,128)(2,1)} %broadcast_in_dim.25), calls=%async_computation.1 | async-start | bytes 524288 | tf_op jit(solution)/shard_map/all_to_all | solution.py:13
  19.1 10.2 %collective-permute-start = (bf16[32,1024]{1,0:T(8,128)(2,1)S(1)}, bf16[32,1024]{1,0:T(8,128)(2,1)S(1)}, u32[]{:S(2)}, u32[]{:S(2)}) collective-permute-start(bf16[32,1024]{1,0:T(8,128)(2,1)S(1)} %get-tuple-element.11), channel_id=1, source_target_pairs={{0,128},{64,192},{128,0},{192,64},{1,129},{65,193},{129,1},{193,65... | collective-permute-start | bytes 196616 | tf_op jit(solution)/shard_map/ppermute | solution.py:52
  23.8 5.5 %collective-permute-start.2 = (bf16[32,1024]{1,0:T(8,128)(2,1)S(1)}, bf16[32,1024]{1,0:T(8,128)(2,1)S(1)}, u32[]{:S(2)}, u32[]{:S(2)}) collective-permute-start(bf16[32,1024]{1,0:T(8,128)(2,1)S(1)} %get-tuple-element.12), channel_id=1, source_target_pairs={{0,192},{64,0},{128,64},{192,128},{1,193},{65,1},{129,65},{193,129... | collective-permute-start | bytes 196616 | tf_op jit(solution)/shard_map/ppermute | solution.py:52
  26.5 6.5 %collective-permute-start.1 = (bf16[32,1024]{1,0:T(8,128)(2,1)S(1)}, bf16[32,1024]{1,0:T(8,128)(2,1)S(1)}, u32[]{:S(2)}, u32[]{:S(2)}) collective-permute-start(bf16[32,1024]{1,0:T(8,128)(2,1)S(1)} %get-tuple-element.13), channel_id=1, source_target_pairs={{0,64},{64,128},{128,192},{192,0},{1,65},{65,129},{129,193},{193,1... | collective-permute-start | bytes 196616 | tf_op jit(solution)/shard_map/ppermute | solution.py:52
  33.1 14.0 %collective-permute-start.3 = (bf16[32,1024]{1,0:T(8,128)(2,1)S(1)}, bf16[32,1024]{1,0:T(8,128)(2,1)S(1)}, u32[]{:S(2)}, u32[]{:S(2)}) collective-permute-start(bf16[32,1024]{1,0:T(8,128)(2,1)S(1)} %fusion.23), channel_id=1, source_target_pairs={{0,256},{256,0},{1,257},{257,1},{2,258},{258,2},{3,259},{259,3},{4... | collective-permute-start | bytes 196616 | tf_op jit(solution)/shard_map/ppermute | solution.py:22
  47.3 8.7 %collective-permute-start.4 = (bf16[2,1,64,1024]{3,2,1,0:T(8,128)(2,1)S(1)}, bf16[2,1,64,1024]{3,2,1,0:T(8,128)(2,1)S(1)}, u32[]{:S(2)}, u32[]{:S(2)}) collective-permute-start(bf16[2,1,64,1024]{3,2,1,0:T(8,128)(2,1)S(1)} %maximum_bitcast_fusion.1), channel_id=1, source_target_pairs={{0,2},{2,0},{1,3},{3,1},{4,6},{6,4},{5,7},{7,5},{8,10},{10,8},{9,1... | collective-permute-start | bytes 786440 | tf_op jit(solution)/shard_map/ppermute | solution.py:22
  51.0 17.2 %all-to-all-start = ((bf16[16,32,1024]{2,1,0:T(8,128)(2,1)}), bf16[16,32,1024]{2,1,0:T(8,128)(2,1)S(1)}, u32[]{:S(2)}, u32[]{:S(2)}) async-start(bf16[16,32,1024]{2,1,0:T(8,128)(2,1)} %broadcast_in_dim.24), calls=%async_computation | async-start | bytes 2097152 | tf_op jit(solution)/shard_map/all_to_all | solution.py:13
  56.1 9.1 %collective-permute-start.5 = (bf16[2,1,2,64,1024]{4,3,2,1,0:T(8,128)(2,1)S(1)}, bf16[2,1,2,64,1024]{4,3,2,1,0:T(8,128)(2,1)}, u32[]{:S(2)}, u32[]{:S(2)}) collective-permute-start(bf16[2,1,2,64,1024]{4,3,2,1,0:T(8,128)(2,1)S(1)} %maximum_bitcast_fusion), channel_id=1, source_target_pairs={{0,1},{1,0},{2,3},{3,2},{4,5},{5,4},{6,7},{7,6},{8,9},{9,8},{10,11... | collective-permute-start | bytes 1572872 | tf_op jit(solution)/shard_map/ppermute | solution.py:22
  69.3 1.7 %copy-start.3 = (bf16[512,512]{1,0:T(8,128)(2,1)}, bf16[512,512]{1,0:T(8,128)(2,1)S(1)}, u32[]{:S(2)}) copy-start(bf16[512,512]{1,0:T(8,128)(2,1)S(1)} %fusion.8) | copy-start | bytes 1572868
  71.0 5.2 %copy-start.4 = (bf16[512,512]{1,0:T(8,128)(2,1)S(1)}, bf16[512,512]{1,0:T(8,128)(2,1)}, u32[]{:S(2)}) copy-start(bf16[512,512]{1,0:T(8,128)(2,1)} %copy-done.3) | copy-start | bytes 1572868
  71.0 20.5 %all-to-all-start.2 = ((bf16[16,32,1024]{2,1,0:T(8,128)(2,1)}), bf16[16,32,1024]{2,1,0:T(8,128)(2,1)S(1)}, u32[]{:S(2)}, u32[]{:S(2)}) async-start(bf16[16,32,1024]{2,1,0:T(8,128)(2,1)} %bitcast.56), calls=%async_computation.2 | async-start | bytes 2097152 | tf_op jit(solution)/shard_map/all_to_all | solution.py:13
  76.6 8.1 %collective-permute-start.6 = (bf16[128,1024]{1,0:T(8,128)(2,1)S(1)}, bf16[128,1024]{1,0:T(8,128)(2,1)S(1)}, u32[]{:S(2)}, u32[]{:S(2)}) collective-permute-start(bf16[128,1024]{1,0:T(8,128)(2,1)S(1)} %slice.49), channel_id=1, source_target_pairs={{0,1},{1,0},{2,3},{3,2},{4,5},{5,4},{6,7},{7,6},{8,9},{9,8},{10,11... | collective-permute-start | bytes 786440 | tf_op jit(solution)/shard_map/ppermute | solution.py:22
  84.8 6.6 %collective-permute-start.7 = (bf16[64,1024]{1,0:T(8,128)(2,1)S(1)}, bf16[64,1024]{1,0:T(8,128)(2,1)S(1)}, u32[]{:S(2)}, u32[]{:S(2)}) collective-permute-start(bf16[64,1024]{1,0:T(8,128)(2,1)S(1)} %slice.50), channel_id=1, source_target_pairs={{0,2},{2,0},{1,3},{3,1},{4,6},{6,4},{5,7},{7,5},{8,10},{10,8},{9,1... | collective-permute-start | bytes 393224 | tf_op jit(solution)/shard_map/ppermute | solution.py:22
  145.8 6.3 %copy-start.1 = (bf16[16,1024]{1,0:T(8,128)(2,1)S(1)}, bf16[16,1024]{1,0:T(8,128)(2,1)}, u32[]{:S(2)}) copy-start(bf16[16,1024]{1,0:T(8,128)(2,1)} %param.7) | copy-start | bytes 98308
  146.7 14.4 %all-to-all-start.6 = ((bf16[16,12,1024]{2,1,0:T(8,128)(2,1)}), bf16[16,12,1024]{2,1,0:T(8,128)(2,1)S(1)}, u32[]{:S(2)}, u32[]{:S(2)}) async-start(bf16[16,12,1024]{2,1,0:T(8,128)(2,1)} %broadcast_in_dim.30), calls=%async_computation.6 | async-start | bytes 1048576 | tf_op jit(solution)/shard_map/all_to_all | solution.py:13
